TPU v7x, 32 devices: a whole 2x2x4 slice. The times are simulated.
32 devices in a mesh: section: 8 (over y, x, core), rep: 4 (over z).
Axes of the slice: x: 2, y: 2, z: 4, core: 2. Of those that a mesh axis runs over, the one named last changes fastest.
Arguments:
- tokens: bfloat16 [8, 4, 256, 1024], P('section', 'rep'), may hold values from -6 to 6
- assign: int32 [8, 4, 256, 1], P('section', 'rep'), may hold values from 0 to 7; in each aligned block of 256 rows (0 to 255, 256 to 511, ..., all dimensions but the last counted through in order) at most 48 rows name the same one
- route_mask: int32 [8], replicated, may hold values from 1 to 3
- match_mask: int32 [8], replicated, may hold values from 1 to 3
- gate_weight: bfloat16 [8, 4, 1024, 256], P('section', 'rep'), may hold values from -0.1875 to 0.1875
- up_weight: bfloat16 [8, 4, 1024, 256], P('section', 'rep'), may hold values from -0.1875 to 0.1875
- down_weight: bfloat16 [8, 4, 256, 1024], P('section', 'rep'), may hold values from -0.375 to 0.375
- slow_down: bfloat16 [8, 4, 256, 1024], P('section', 'rep'), may hold values from -4 to 4
- momentum: bfloat16 [8, 4, 256, 1024], P('section', 'rep'), may hold values from -4 to 4
- slot_cot: bfloat16 [8, 4, 8, 48, 1024], P('section', 'rep'), may hold values from -6 to 6
Outputs:
- input_grad: bfloat16 [8, 4, 256, 1024], P('section', 'rep')
- new_slow: bfloat16 [8, 4, 256, 1024], P('section', 'rep')
Inputs may be any that keep to these rules, and one draw needn't show every extreme that they name: `assign`: no expert is named by more than 48 rows of one device, and in every draw some device has 48 rows for one expert. Rows that replica r of any section sends to expert e are processed by replica r XOR route_mask[e] of that expert. Replica r of section s is matched with replica r XOR match_mask[s].
All inputs are finite; a program needn't handle non-finite values.
Results may differ from a plain program's by a relative error of at most 0.012.
Values may be sent and summed in bfloat16 or wider, within the bound.
No kernel may reach another device: no remote copies, remote signals or barrier semaphores. Data moves between devices by JAX's collectives and lax.ppermute only.
A program may use at most 64 MiB of HBM per device.

v0:
```python
import jax
import jax.numpy as jnp
from jax import lax
from jax.sharding import PartitionSpec as P

inner_rate = 0.05
pull_rate = 0.25
moment_rate = 0.9
outer_rate = 0.7

OUTWARD = [(1, 0), (2, 3)]
INWARD = [(0, 1), (3, 2)]
ACROSS = [(1, 2), (2, 1)]


def from_partner(value, distance):
    pairs = [(source, source ^ 2**distance) for source in range(lax.axis_size("rep"))]
    return lax.ppermute(value, "rep", pairs)


def bit_of(mask, index):
    return jnp.bitwise_and(jnp.right_shift(mask, index), 1) == 1


def route(value, mask, bits):
    for index in bits:
        value = jnp.where(bit_of(mask, index), from_partner(value, index), value)
    return value


def after(value, *earlier):
    return lax.optimization_barrier((value, *earlier))[0]


def slot_table(expert_ids, sections, capacity):
    expert_hot = (expert_ids[:, None] == jnp.arange(sections, dtype=jnp.int32)[None, :]).astype(
        jnp.int32
    )
    position = jnp.sum((jnp.cumsum(expert_hot, axis=0) - 1) * expert_hot, axis=1)
    slot_index = expert_ids * capacity + position
    return (
        slot_index[:, None] == jnp.arange(sections * capacity, dtype=jnp.int32)[None, :]
    ).astype(jnp.bfloat16)


def stacked(wide, width):
    return jnp.concatenate(jnp.split(wide, wide.shape[1] // width, axis=1), axis=0)


def side_by_side(tall):
    return jnp.concatenate(jnp.split(tall, tall.shape[0] // tall.shape[1], axis=0), axis=1)


class FourInLine:
    def __init__(self, gate, up, down, static_part, mask):
        replica = lax.axis_index("rep")
        self.inner = (replica == 1) | (replica == 2)
        self.near, self.far = mask == 1, mask == 3
        self.gate, self.up, self.down = gate, up, down
        self.static_part = static_part

    def forward(self, bits):
        self.up_side = lax.ppermute(self.up, "rep", INWARD)
        self.gate_hub = lax.ppermute(self.gate, "rep", ACROSS)
        inner, self.near, self.far, *bits = lax.optimization_barrier(
            (self.inner, self.near, self.far, *bits)
        )
        send = lax.optimization_barrier(jnp.where(inner, self.static_part, self.gate))
        self.one = from_partner(send, 0)
        side, self.near, self.far = lax.optimization_barrier((self.up_side, self.near, self.far))
        first = jnp.where(self.far, side, self.up)
        second = jnp.where(self.far, self.up, side)
        first_in = lax.ppermute(first, "rep", ACROSS)
        self.quiet, self.first_in = first, first_in
        self.gate_edge = lax.ppermute(self.one, "rep", ACROSS)
        self.second = second
        return bits

    def handed_up(self, earlier):
        first_in = after(self.first_in, *earlier)
        send = jnp.where(self.inner, jnp.where(self.near, self.up, first_in), self.down)
        self.two = from_partner(send, 0)
        self.up_hub = lax.ppermute(after(self.second, send), "rep", ACROSS)
        self.later = send

    def handed_gate(self, earlier):
        gate_edge = after(self.gate_edge, self.later, *earlier)
        gate_out = jnp.where(
            self.near, self.gate, jnp.where(self.far, gate_edge, self.gate_hub)
        )
        send = jnp.where(self.inner, gate_out, self.static_part)
        self.three = from_partner(send, 0)
        two = after(self.two, send)
        first = jnp.where(self.far, two, self.down)
        second = jnp.where(self.far, self.down, two)
        self.down_first = lax.ppermute(first, "rep", ACROSS)
        gate_in = jnp.where(
            self.near, self.one, jnp.where(self.far, self.gate_hub, self.gate_edge)
        )
        two, up_hub = lax.optimization_barrier((two, self.up_hub, first))[:2]
        self.second_down = second
        up_in = jnp.where(self.near, self.up_side, up_hub)
        self.gate_in = gate_in
        return jnp.where(self.inner, up_in, two)

    def gate_here(self, earlier):
        three = after(self.three, *earlier)
        static_in = jnp.where(self.inner, three, self.one)
        return lax.optimization_barrier(jnp.where(self.inner, self.gate_in, three)), static_in

    def swap_down(self, earlier):
        second = after(self.second_down, *earlier)
        self.down_hub = lax.ppermute(second, "rep", ACROSS)

    def handed_down(self, earlier):
        send = jnp.where(self.near, self.down, after(self.down_first, *earlier))
        self.four = lax.ppermute(send, "rep", OUTWARD)
        return send

    def down_here(self, earlier):
        down_hub = after(self.down_hub, *earlier)
        down_in = jnp.where(self.near, self.two, down_hub)
        return jnp.where(self.inner, down_in, self.four)


def on_device(
    tokens,
    assign,
    route_mask,
    match_mask,
    gate_weight,
    up_weight,
    down_weight,
    slow_down,
    momentum,
    slot_cot,
):
    sections = lax.axis_size("section")
    levels = lax.axis_size("rep").bit_length() - 1
    section_here = lax.axis_index("section")
    token_rows = tokens[0, 0]
    expert_ids = assign[0, 0, :, 0]
    capacity = slot_cot.shape[3]
    model_width = token_rows.shape[1]
    masks_here = lax.dynamic_index_in_dim(
        jnp.stack([route_mask, match_mask]), section_here, axis=1, keepdims=False
    )
    own_mask, match = masks_here[0], masks_here[1]
    match_mine = jnp.bitwise_xor(own_mask, match)
    upward = list(range(levels))
    bits = [bit_of(mask, index) for mask in (own_mask, match_mine, match) for index in upward]
    contract = (((1,), (1,)), ((), ()))
    hidden_width = gate_weight.shape[3]

    gate_raw, up_raw, down_raw = gate_weight[0, 0], up_weight[0, 0], down_weight[0, 0]
    slow_float = slow_down[0, 0].astype(jnp.float32)
    down_float = down_raw.astype(jnp.float32)
    static_part = ((0.5 - pull_rate) * slow_float - 0.5 * down_float).astype(jnp.bfloat16)

    selector = slot_table(expert_ids, sections, capacity)
    placed = lax.dot_general(
        selector, token_rows, (((0,), (0,)), ((), ())), preferred_element_type=jnp.float32
    )
    dispatched = placed.astype(jnp.bfloat16).reshape(sections, capacity, model_width)

    line = None
    if levels == 2:
        line = FourInLine(
            gate_raw,
            up_raw,
            stacked(down_raw, hidden_width),
            stacked(lax.optimization_barrier(static_part), hidden_width),
            own_mask,
        )
        bits = line.forward(bits)
        dispatched, line.gate_hub = lax.optimization_barrier(
            (dispatched, line.gate_hub, line.quiet)
        )[:2]
        line.handed_up((dispatched,))
    arrived = lax.all_to_all(dispatched, "section", split_axis=0, concat_axis=0, tiled=True)
    rows = arrived.reshape(-1, model_width)
    cotangent = slot_cot[0, 0].reshape(-1, model_width)
    if line is not None:
        up_mat = line.handed_gate((rows,))
    else:
        gate_mat, up_mat, down_mat = [
            route(weight, own_mask, upward) for weight in (gate_raw, up_raw, down_raw)
        ]
        static_in = from_partner(static_part, 0)

    up_act = jnp.dot(rows, up_mat, preferred_element_type=jnp.float32)
    if line is not None:
        gate_mat, static_in = line.gate_here((up_act,))
        static_in = side_by_side(static_in)
    gate_act = jnp.dot(rows, gate_mat, preferred_element_type=jnp.float32)
    sigmoid_gate = jax.nn.sigmoid(gate_act)
    hidden = (gate_act * sigmoid_gate * up_act).astype(jnp.bfloat16)
    down_grad = lax.dot_general(
        hidden, cotangent, (((0,), (0,)), ((), ())), preferred_element_type=jnp.float32
    ).astype(jnp.bfloat16)

    if line is not None:
        line.swap_down((down_grad,))

    own_bits, mine_bits, match_bits = [
        bits[number * levels : (number + 1) * levels] for number in range(3)
    ]
    lower, top = upward[:-1], levels - 1
    down_grad_in = from_partner(down_grad, 0)
    if line is not None:
        sent = line.handed_down((down_grad,))
        static_in = after(static_in, sent)
        down_grad_in = after(down_grad_in, static_in)
    own_routed, match_routed, static_routed = down_grad, down_grad, static_part
    for index in lower:
        if index == 0:
            own_in, match_in, static_here = down_grad_in, down_grad_in, static_in
        else:
            own_in = from_partner(own_routed, index)
            match_in = from_partner(match_routed, index)
            static_here = from_partner(static_routed, index)
        own_routed = jnp.where(own_bits[index], own_in, own_routed)
        match_routed = jnp.where(mine_bits[index], match_in, match_routed)
        static_routed = jnp.where(match_bits[index], static_here, static_routed)

    def combined(side, static_routed, own_routed, match_routed):
        def pick(bit, value):
            return jnp.where(bit == side, value.astype(jnp.float32), 0.0)

        return pick(match_bits[top], static_routed) + 0.5 * inner_rate * (
            pick(own_bits[top], own_routed) + pick(mine_bits[top], match_routed)
        )

    crossing_out = combined(True, static_routed, own_routed, match_routed).astype(jnp.bfloat16)
    if line is not None:
        crossing_out = after(crossing_out, line.down_hub)
    crossing = from_partner(crossing_out, top)
    slow_float = after(slow_down[0, 0], crossing_out).astype(jnp.float32)
    staying = combined(False, static_routed, own_routed, match_routed)
    outer_here = (0.5 + pull_rate) * slow_float - 0.5 * down_float + staying
    pull = outer_rate * (1.0 + moment_rate)
    kept = (
        slow_float
        - pull * outer_here
        - (outer_rate * moment_rate * moment_rate) * momentum[0, 0].astype(jnp.float32)
    )
    kept = after(kept, crossing_out)
    new_slow = (kept - pull * crossing.astype(jnp.float32)).astype(jnp.bfloat16)

    if line is not None:
        down_mat = side_by_side(line.down_here((crossing_out,)))
    hidden_grad = lax.dot_general(
        cotangent, down_mat, contract, preferred_element_type=jnp.float32
    )
    gate_grad = (
        hidden_grad * up_act * sigmoid_gate * (1.0 + gate_act * (1.0 - sigmoid_gate))
    ).astype(jnp.bfloat16)
    up_grad = (hidden_grad * gate_act * sigmoid_gate).astype(jnp.bfloat16)
    slot_grad = (
        lax.dot_general(gate_grad, gate_mat, contract, preferred_element_type=jnp.float32)
        + lax.dot_general(up_grad, up_mat, contract, preferred_element_type=jnp.float32)
    ).astype(jnp.bfloat16)
    slot_grad = slot_grad.reshape(sections, capacity, model_width)
    returned = lax.all_to_all(slot_grad, "section", split_axis=0, concat_axis=0, tiled=True)
    input_grad = jnp.dot(
        selector, returned.reshape(-1, model_width), preferred_element_type=jnp.float32
    ).astype(jnp.bfloat16)
    return (input_grad[None, None], new_slow[None, None])


def solution(mesh):
    in_specs = (
        P("section", "rep", None, None),
        P("section", "rep", None, None),
        P(),
        P(),
        P("section", "rep", None, None),
        P("section", "rep", None, None),
        P("section", "rep", None, None),
        P("section", "rep", None, None),
        P("section", "rep", None, None),
        P("section", "rep", None, None, None),
    )
    out_specs = (P("section", "rep", None, None), P("section", "rep", None, None))
    return jax.shard_map(
        on_device, mesh=mesh, in_specs=in_specs, out_specs=out_specs, check_vma=False
    )
```

profile of v0, /device:TPU:0, one launch (start us, length us, event | category | flops | bytes accessed | tf_op | source)
XLA Modules:
  0.0 108.5 jit_solution(11028953166139829928)
XLA Ops:
  0.7 5.1 %collective-permute-start = (bf16[1024,256]{1,0:T(8,128)(2,1)}, bf16[1024,256]{1,0:T(8,128)(2,1)S(1)}, u32[]{:S(2)}, u32[]{:S(2)}) collective-permute-start(bf16[1024,256]{1,0:T(8,128)(2,1)} %bitcast.63), channel_id=1, source_target_pairs={{0,1},{3,2},{4,5},{7,6},{8,9},{11,10},{12,13},{15,14},{16,17},{19,... | collective-permute-start | bytes 1572872 | tf_op jit(solution)/shard_map/ppermute | solution.py:63
  5.8 1.5 %collective-permute-start.2 = (bf16[1024,256]{1,0:T(8,128)(2,1)}, bf16[1024,256]{1,0:T(8,128)(2,1)}, u32[]{:S(2)}, u32[]{:S(2)}) collective-permute-start(bf16[1024,256]{1,0:T(8,128)(2,1)} %bitcast.64), channel_id=1, source_target_pairs={{1,2},{2,1},{5,6},{6,5},{9,10},{10,9},{13,14},{14,13},{17,18},{18,... | collective-permute-start | bytes 1572872 | tf_op jit(solution)/shard_map/ppermute | solution.py:64
  13.7 1.4 %subtract_convert_fusion.1 = bf16[256,1024]{1,0:T(8,128)(2,1)S(1)} fusion(bf16[1,1,256,1024]{3,2,1,0:T(8,128)(2,1)} %param.17, bf16[1,1,256,1024]{3,2,1,0:T(8,128)(2,1)} %param.16), kind=kLoop, calls=%fused_computation.26 | loop fusion | flops 1572864 | bytes 1572864 | tf_op jit(solution)/shard_map/convert_element_type | solution.py:158
  16.2 1.4 %collective-permute-start.4 = (bf16[1024,256]{1,0:T(8,128)(2,1)}, bf16[1024,256]{1,0:T(8,128)(2,1)}, u32[]{:S(2)}, u32[]{:S(2)}) collective-permute-start(bf16[1024,256]{1,0:T(8,128)(2,1)} %broadcast_select_fusion.3), channel_id=1, source_target_pairs={{0,1},{1,0},{2,3},{3,2},{4,5},{5,4},{6,7},{7,6},{8,9},{9,8},{10,11... | collective-permute-start | bytes 1572872 | tf_op jit(solution)/shard_map/ppermute | solution.py:18
  19.7 1.6 %collective-permute-start.1 = (bf16[1024,256]{1,0:T(8,128)(2,1)}, bf16[1024,256]{1,0:T(8,128)(2,1)}, u32[]{:S(2)}, u32[]{:S(2)}) collective-permute-start(bf16[1024,256]{1,0:T(8,128)(2,1)} %get-tuple-element.65), channel_id=1, source_target_pairs={{1,2},{2,1},{5,6},{6,5},{9,10},{10,9},{13,14},{14,13},{17,18},{18,... | collective-permute-start | bytes 1572872 | tf_op jit(solution)/shard_map/ppermute | solution.py:73
  21.3 2.4 %convolution_convert_fusion = bf16[384,1024]{1,0:T(8,128)(2,1)} fusion(bf16[1,1,256,1024]{3,2,1,0:T(8,128)(2,1)} %param.10, s32[256]{0:T(256)S(1)} %multiply_add_fusion), kind=kOutput, calls=%fused_computation.1 | convolution fusion | flops 201818112 | bytes 1311744 | tf_op jit(solution)/shard_map/dot_general | solution.py:161
  23.7 3.7 %all-to-all-start = ((bf16[8,48,1024]{2,1,0:T(8,128)(2,1)}), bf16[8,48,1024]{2,1,0:T(8,128)(2,1)S(1)}, u32[]{:S(2)}, u32[]{:S(2)}) async-start(bf16[8,48,1024]{2,1,0:T(8,128)(2,1)} %bitcast.16), calls=%async_computation | async-start | bytes 1572864 | tf_op jit(solution)/shard_map/all_to_all | solution.py:180
  27.4 2.4 %collective-permute-done.4 = bf16[1024,256]{1,0:T(8,128)(2,1)} collective-permute-done((bf16[1024,256]{1,0:T(8,128)(2,1)}, bf16[1024,256]{1,0:T(8,128)(2,1)}, u32[]{:S(2)}, u32[]{:S(2)}) %collective-permute-start.4) | collective-permute-done | bytes 524320 | tf_op jit(solution)/shard_map/ppermute | solution.py:18
  29.9 1.5 %collective-permute-start.5 = (bf16[1024,256]{1,0:T(8,128)(2,1)}, bf16[1024,256]{1,0:T(8,128)(2,1)}, u32[]{:S(2)}, u32[]{:S(2)}) collective-permute-start(bf16[1024,256]{1,0:T(8,128)(2,1)} %collective-permute-done.4), channel_id=1, source_target_pairs={{1,2},{2,1},{5,6},{6,5},{9,10},{10,9},{13,14},{14,13},{17,18},{18,... | collective-permute-start | bytes 1572872 | tf_op jit(solution)/shard_map/ppermute | solution.py:75
  32.4 4.6 %collective-permute-start.3 = (bf16[1024,256]{1,0:T(8,128)(2,1)}, bf16[1024,256]{1,0:T(8,128)(2,1)S(1)}, u32[]{:S(2)}, u32[]{:S(2)}) collective-permute-start(bf16[1024,256]{1,0:T(8,128)(2,1)} %select_select_fusion.4), channel_id=1, source_target_pairs={{0,1},{1,0},{2,3},{3,2},{4,5},{5,4},{6,7},{7,6},{8,9},{9,8},{10,11... | collective-permute-start | bytes 1572872 | tf_op jit(solution)/shard_map/ppermute | solution.py:18
  37.0 1.5 %collective-permute-start.7 = (bf16[1024,256]{1,0:T(8,128)(2,1)}, bf16[1024,256]{1,0:T(8,128)(2,1)}, u32[]{:S(2)}, u32[]{:S(2)}) collective-permute-start(bf16[1024,256]{1,0:T(8,128)(2,1)} %get-tuple-element.42), channel_id=1, source_target_pairs={{1,2},{2,1},{5,6},{6,5},{9,10},{10,9},{13,14},{14,13},{17,18},{18,... | collective-permute-start | bytes 1572872 | tf_op jit(solution)/shard_map/ppermute | solution.py:83
  38.4 1.6 %all-to-all-done = bf16[8,48,1024]{2,1,0:T(8,128)(2,1)S(1)} async-done(((bf16[8,48,1024]{2,1,0:T(8,128)(2,1)}), bf16[8,48,1024]{2,1,0:T(8,128)(2,1)S(1)}, u32[]{:S(2)}, u32[]{:S(2)}) %all-to-all-start) | async-done | bytes 786464 | tf_op jit(solution)/shard_map/all_to_all | solution.py:180
  40.0 1.7 %select_select_fusion.3 = bf16[1024,256]{1,0:T(8,128)(2,1)S(1)} fusion(bf16[1024,256]{1,0:T(8,128)(2,1)} %collective-permute-done.5, bf16[1024,256]{1,0:T(8,128)(2,1)} %collective-permute-done.2, pred[]{:T(512)} %bitcast.8, pred[]{:T(512)} %bitcast.7, pred[]{:T(512)S(6)} %or.3, bf16[256,256]{1,0:T(8,128)(2,1)} %copy-done.11, bf16[256,256]{1,0:T(8,128)(2,1)} %copy-done.12, ...), kind=kLoop, calls=%fused_computation.43 | loop fusion | flops 2883584 | bytes 2621443 | tf_op jit(solution)/shard_map/jit(_where)/select_n | solution.py:91
  41.7 8.2 %collective-permute-start.6 = (bf16[1024,256]{1,0:T(8,128)(2,1)S(1)}, bf16[1024,256]{1,0:T(8,128)(2,1)S(1)}, u32[]{:S(2)}, u32[]{:S(2)}) collective-permute-start(bf16[1024,256]{1,0:T(8,128)(2,1)S(1)} %select_select_fusion.3), channel_id=1, source_target_pairs={{0,1},{1,0},{2,3},{3,2},{4,5},{5,4},{6,7},{7,6},{8,9},{9,8},{10,11... | collective-permute-start | bytes 1572872 | tf_op jit(solution)/shard_map/ppermute | solution.py:18
  51.3 10.0 %collective-permute-done.6 = bf16[1024,256]{1,0:T(8,128)(2,1)S(1)} collective-permute-done((bf16[1024,256]{1,0:T(8,128)(2,1)S(1)}, bf16[1024,256]{1,0:T(8,128)(2,1)S(1)}, u32[]{:S(2)}, u32[]{:S(2)}) %collective-permute-start.6) | collective-permute-done | bytes 524320 | tf_op jit(solution)/shard_map/ppermute | solution.py:18
  63.6 1.8 %collective-permute-start.10 = (bf16[256,1024]{1,0:T(8,128)(2,1)S(1)}, bf16[256,1024]{1,0:T(8,128)(2,1)S(1)}, u32[]{:S(2)}, u32[]{:S(2)}) collective-permute-start(bf16[256,1024]{1,0:T(8,128)(2,1)S(1)} %convolution_convert_fusion.2), channel_id=1, source_target_pairs={{0,1},{1,0},{2,3},{3,2},{4,5},{5,4},{6,7},{7,6},{8,9},{9,8},{10,11... | collective-permute-start | bytes 1572872 | tf_op jit(solution)/shard_map/ppermute | solution.py:18
  67.6 10.9 %collective-permute-done.10 = bf16[256,1024]{1,0:T(8,128)(2,1)S(1)} collective-permute-done((bf16[256,1024]{1,0:T(8,128)(2,1)S(1)}, bf16[256,1024]{1,0:T(8,128)(2,1)S(1)}, u32[]{:S(2)}, u32[]{:S(2)}) %collective-permute-start.10) | collective-permute-done | bytes 524320 | tf_op jit(solution)/shard_map/ppermute | solution.py:18
  79.8 2.0 %collective-permute-start.12 = (bf16[256,1024]{1,0:T(8,128)(2,1)}, bf16[256,1024]{1,0:T(8,128)(2,1)}, u32[]{:S(2)}, u32[]{:S(2)}) collective-permute-start(bf16[256,1024]{1,0:T(8,128)(2,1)} %fusion.2), channel_id=1, source_target_pairs={{0,2},{1,3},{2,0},{3,1},{4,6},{5,7},{6,4},{7,5},{8,10},{9,11},{10,... | collective-permute-start | bytes 1572872 | tf_op jit(solution)/shard_map/ppermute | solution.py:18
  81.8 7.0 %collective-permute-done.11 = bf16[1024,256]{1,0:T(8,128)(2,1)S(1)} collective-permute-done((bf16[1024,256]{1,0:T(8,128)(2,1)S(1)}, bf16[1024,256]{1,0:T(8,128)(2,1)S(1)}, u32[]{:S(2)}, u32[]{:S(2)}) %collective-permute-start.11) | collective-permute-done | bytes 524320 | tf_op jit(solution)/shard_map/ppermute | solution.py:117
  89.8 1.4 %add_convert_fusion = bf16[384,1024]{1,0:T(8,128)(2,1)} fusion(f32[384,1024]{1,0:T(8,128)S(1)} %fusion.21, bf16[1024,256]{1,0:T(8,128)(2,1)S(1)} %get-tuple-element.61, f32[384,256]{1,0:T(8,128)S(1)} %fusion.39, f32[384,256]{1,0:T(8,128)S(1)} %convolution_bitcast_fusion, f32[384,256]{1,0:T(8,128)S(1)} %fusion.38), kind=kOutput, calls=%fused_computation | convolution fusion | flops 203096064 | bytes 4063232 | tf_op jit(solution)/shard_map/dot_general | solution.py:260
  91.2 3.5 %all-to-all-start.1 = ((bf16[8,48,1024]{2,1,0:T(8,128)(2,1)}), bf16[8,48,1024]{2,1,0:T(8,128)(2,1)S(1)}, u32[]{:S(2)}, u32[]{:S(2)}) async-start(bf16[8,48,1024]{2,1,0:T(8,128)(2,1)} %bitcast.61), calls=%async_computation.1 | async-start | bytes 1572864 | tf_op jit(solution)/shard_map/all_to_all | solution.py:264
  94.7 2.4 %fusion.11 = f32[256,1024]{1,0:T(8,128)S(1)} fusion(bf16[256,1024]{1,0:T(8,128)(2,1)} %bitcast.62, bf16[1,1,256,1024]{3,2,1,0:T(8,128)(2,1)} %param.18, pred[]{:T(512)S(6)} %eq.129, pred[]{:T(512)S(6)} %eq.128, pred[]{:T(512)S(6)} %eq.127, bf16[256,1024]{1,0:T(8,128)(2,1)S(1)} %pad_maximum_fusion.2, bf16[256,1024]{1,0:T(8,128)(2,1)S(1)} %subtract_convert_fusion.1, ...), kind=kLoop, calls=%fused_computation.24 | loop fusion | flops 6029312 | bytes 4718598 | tf_op jit(solution)/shard_map/sub | solution.py:243
  97.1 7.7 %collective-permute-done.12 = bf16[256,1024]{1,0:T(8,128)(2,1)} collective-permute-done((bf16[256,1024]{1,0:T(8,128)(2,1)}, bf16[256,1024]{1,0:T(8,128)(2,1)}, u32[]{:S(2)}, u32[]{:S(2)}) %collective-permute-start.12) | collective-permute-done | bytes 524320 | tf_op jit(solution)/shard_map/ppermute | solution.py:18
  104.8 2.0 %fusion.12 = bf16[1,1,256,1024]{3,2,1,0:T(8,128)(2,1)} fusion(f32[256,1024]{1,0:T(8,128)S(1)} %fusion.11, bf16[256,1024]{1,0:T(8,128)(2,1)} %collective-permute-done.12), kind=kLoop, calls=%fused_computation.28 | loop fusion | flops 1048576 | bytes 2097152 | tf_op jit(solution)/shard_map/broadcast_in_dim | solution.py:268
  (72 shorter events, 15.2 us)
Async XLA Ops:
  0.6 62.4 %copy-start = (bf16[1,1,8,48,1024]{4,3,2,1,0:T(8,128)(2,1)S(1)}, bf16[1,1,8,48,1024]{4,3,2,1,0:T(8,128)(2,1)}, u32[]{:S(2)}) copy-start(bf16[1,1,8,48,1024]{4,3,2,1,0:T(8,128)(2,1)} %param.19) | copy-start | bytes 2359300
  0.6 14.6 %copy-start.7 = (bf16[1,1,1024,256]{3,2,1,0:T(8,128)(2,1)S(1)}, bf16[1,1,1024,256]{3,2,1,0:T(8,128)(2,1)}, u32[]{:S(2)}) copy-start(bf16[1,1,1024,256]{3,2,1,0:T(8,128)(2,1)} %param.14) | copy-start | bytes 1572868
  0.7 17.8 %collective-permute-start = (bf16[1024,256]{1,0:T(8,128)(2,1)}, bf16[1024,256]{1,0:T(8,128)(2,1)S(1)}, u32[]{:S(2)}, u32[]{:S(2)}) collective-permute-start(bf16[1024,256]{1,0:T(8,128)(2,1)} %bitcast.63), channel_id=1, source_target_pairs={{0,1},{3,2},{4,5},{7,6},{8,9},{11,10},{12,13},{15,14},{16,17},{19,... | collective-permute-start | bytes 1572872 | tf_op jit(solution)/shard_map/ppermute | solution.py:63
  5.8 17.9 %collective-permute-start.2 = (bf16[1024,256]{1,0:T(8,128)(2,1)}, bf16[1024,256]{1,0:T(8,128)(2,1)}, u32[]{:S(2)}, u32[]{:S(2)}) collective-permute-start(bf16[1024,256]{1,0:T(8,128)(2,1)} %bitcast.64), channel_id=1, source_target_pairs={{1,2},{2,1},{5,6},{6,5},{9,10},{10,9},{13,14},{14,13},{17,18},{18,... | collective-permute-start | bytes 1572872 | tf_op jit(solution)/shard_map/ppermute | solution.py:64
  16.2 13.7 %collective-permute-start.4 = (bf16[1024,256]{1,0:T(8,128)(2,1)}, bf16[1024,256]{1,0:T(8,128)(2,1)}, u32[]{:S(2)}, u32[]{:S(2)}) collective-permute-start(bf16[1024,256]{1,0:T(8,128)(2,1)} %broadcast_select_fusion.3), channel_id=1, source_target_pairs={{0,1},{1,0},{2,3},{3,2},{4,5},{5,4},{6,7},{7,6},{8,9},{9,8},{10,11... | collective-permute-start | bytes 1572872 | tf_op jit(solution)/shard_map/ppermute | solution.py:18
  18.5 5.2 %copy-start.3 = (bf16[1024,256]{1,0:T(8,128)(2,1)}, bf16[1024,256]{1,0:T(8,128)(2,1)S(1)}, u32[]{:S(2)}) copy-start(bf16[1024,256]{1,0:T(8,128)(2,1)S(1)} %collective-permute-done) | copy-start | bytes 1572868
  19.7 11.7 %copy-start.1 = (bf16[1,1,256,1024]{3,2,1,0:T(8,128)(2,1)S(1)}, bf16[1,1,256,1024]{3,2,1,0:T(8,128)(2,1)}, u32[]{:S(2)}) copy-start(bf16[1,1,256,1024]{3,2,1,0:T(8,128)(2,1)} %param.16) | copy-start | bytes 1572868
  19.7 11.7 %collective-permute-start.1 = (bf16[1024,256]{1,0:T(8,128)(2,1)}, bf16[1024,256]{1,0:T(8,128)(2,1)}, u32[]{:S(2)}, u32[]{:S(2)}) collective-permute-start(bf16[1024,256]{1,0:T(8,128)(2,1)} %get-tuple-element.65), channel_id=1, source_target_pairs={{1,2},{2,1},{5,6},{6,5},{9,10},{10,9},{13,14},{14,13},{17,18},{18,... | collective-permute-start | bytes 1572872 | tf_op jit(solution)/shard_map/ppermute | solution.py:73
  23.7 16.3 %all-to-all-start = ((bf16[8,48,1024]{2,1,0:T(8,128)(2,1)}), bf16[8,48,1024]{2,1,0:T(8,128)(2,1)S(1)}, u32[]{:S(2)}, u32[]{:S(2)}) async-start(bf16[8,48,1024]{2,1,0:T(8,128)(2,1)} %bitcast.16), calls=%async_computation | async-start | bytes 1572864 | tf_op jit(solution)/shard_map/all_to_all | solution.py:180
  29.9 8.6 %collective-permute-start.5 = (bf16[1024,256]{1,0:T(8,128)(2,1)}, bf16[1024,256]{1,0:T(8,128)(2,1)}, u32[]{:S(2)}, u32[]{:S(2)}) collective-permute-start(bf16[1024,256]{1,0:T(8,128)(2,1)} %collective-permute-done.4), channel_id=1, source_target_pairs={{1,2},{2,1},{5,6},{6,5},{9,10},{10,9},{13,14},{14,13},{17,18},{18,... | collective-permute-start | bytes 1572872 | tf_op jit(solution)/shard_map/ppermute | solution.py:75
  31.4 7.1 %copy-start.8 = (bf16[256,256]{1,0:T(8,128)(2,1)}, bf16[256,256]{1,0:T(8,128)(2,1)S(1)}, u32[]{:S(2)}) copy-start(bf16[256,256]{1,0:T(8,128)(2,1)S(1)} %get-tuple-element.81) | copy-start | bytes 393220
  32.4 17.5 %collective-permute-start.3 = (bf16[1024,256]{1,0:T(8,128)(2,1)}, bf16[1024,256]{1,0:T(8,128)(2,1)S(1)}, u32[]{:S(2)}, u32[]{:S(2)}) collective-permute-start(bf16[1024,256]{1,0:T(8,128)(2,1)} %select_select_fusion.4), channel_id=1, source_target_pairs={{0,1},{1,0},{2,3},{3,2},{4,5},{5,4},{6,7},{7,6},{8,9},{9,8},{10,11... | collective-permute-start | bytes 1572872 | tf_op jit(solution)/shard_map/ppermute | solution.py:18
  37.0 13.8 %collective-permute-start.7 = (bf16[1024,256]{1,0:T(8,128)(2,1)}, bf16[1024,256]{1,0:T(8,128)(2,1)}, u32[]{:S(2)}, u32[]{:S(2)}) collective-permute-start(bf16[1024,256]{1,0:T(8,128)(2,1)} %get-tuple-element.42), channel_id=1, source_target_pairs={{1,2},{2,1},{5,6},{6,5},{9,10},{10,9},{13,14},{14,13},{17,18},{18,... | collective-permute-start | bytes 1572872 | tf_op jit(solution)/shard_map/ppermute | solution.py:83
  40.0 9.9 %copy-start.9 = (bf16[256,256]{1,0:T(8,128)(2,1)S(1)}, bf16[256,256]{1,0:T(8,128)(2,1)}, u32[]{:S(2)}) copy-start(bf16[256,256]{1,0:T(8,128)(2,1)} %copy-done.8) | copy-start | bytes 393220
  41.7 9.1 %copy-start.4 = (bf16[1024,256]{1,0:T(8,128)(2,1)S(1)}, bf16[1024,256]{1,0:T(8,128)(2,1)}, u32[]{:S(2)}) copy-start(bf16[1024,256]{1,0:T(8,128)(2,1)} %copy-done.3) | copy-start | bytes 1572868
  41.7 19.6 %collective-permute-start.6 = (bf16[1024,256]{1,0:T(8,128)(2,1)S(1)}, bf16[1024,256]{1,0:T(8,128)(2,1)S(1)}, u32[]{:S(2)}, u32[]{:S(2)}) collective-permute-start(bf16[1024,256]{1,0:T(8,128)(2,1)S(1)} %select_select_fusion.3), channel_id=1, source_target_pairs={{0,1},{1,0},{2,3},{3,2},{4,5},{5,4},{6,7},{7,6},{8,9},{9,8},{10,11... | collective-permute-start | bytes 1572872 | tf_op jit(solution)/shard_map/ppermute | solution.py:18
  50.1 16.0 %collective-permute-start.9 = (bf16[1024,256]{1,0:T(8,128)(2,1)S(1)}, bf16[1024,256]{1,0:T(8,128)(2,1)S(1)}, u32[]{:S(2)}, u32[]{:S(2)}) collective-permute-start(bf16[1024,256]{1,0:T(8,128)(2,1)S(1)} %get-tuple-element.63), channel_id=1, source_target_pairs={{1,2},{2,1},{5,6},{6,5},{9,10},{10,9},{13,14},{14,13},{17,18},{18,... | collective-permute-start | bytes 1572872 | tf_op jit(solution)/shard_map/ppermute | solution.py:96
  63.6 25.4 %copy-start.5 = (bf16[256,1024]{1,0:T(8,128)(2,1)}, bf16[256,1024]{1,0:T(8,128)(2,1)S(1)}, u32[]{:S(2)}) copy-start(bf16[256,1024]{1,0:T(8,128)(2,1)S(1)} %convolution_convert_fusion.2) | copy-start | bytes 1572868
  63.6 14.9 %collective-permute-start.10 = (bf16[256,1024]{1,0:T(8,128)(2,1)S(1)}, bf16[256,1024]{1,0:T(8,128)(2,1)S(1)}, u32[]{:S(2)}, u32[]{:S(2)}) collective-permute-start(bf16[256,1024]{1,0:T(8,128)(2,1)S(1)} %convolution_convert_fusion.2), channel_id=1, source_target_pairs={{0,1},{1,0},{2,3},{3,2},{4,5},{5,4},{6,7},{7,6},{8,9},{9,8},{10,11... | collective-permute-start | bytes 1572872 | tf_op jit(solution)/shard_map/ppermute | solution.py:18
  65.4 14.4 %collective-permute-start.8 = (bf16[1024,256]{1,0:T(8,128)(2,1)S(1)}, bf16[1024,256]{1,0:T(8,128)(2,1)S(1)}, u32[]{:S(2)}, u32[]{:S(2)}) collective-permute-start(bf16[1024,256]{1,0:T(8,128)(2,1)S(1)} %get-tuple-element.46), channel_id=1, source_target_pairs={{1,2},{2,1},{5,6},{6,5},{9,10},{10,9},{13,14},{14,13},{17,18},{18,... | collective-permute-start | bytes 1572872 | tf_op jit(solution)/shard_map/ppermute | solution.py:113
  66.2 22.6 %collective-permute-start.11 = (bf16[1024,256]{1,0:T(8,128)(2,1)S(1)}, bf16[1024,256]{1,0:T(8,128)(2,1)S(1)}, u32[]{:S(2)}, u32[]{:S(2)}) collective-permute-start(bf16[1024,256]{1,0:T(8,128)(2,1)S(1)} %broadcast_select_fusion.8), channel_id=1, source_target_pairs={{1,0},{2,3},{5,4},{6,7},{9,8},{10,11},{13,12},{14,15},{17,16},{18,... | collective-permute-start | bytes 1572872 | tf_op jit(solution)/shard_map/ppermute | solution.py:117
  78.5 10.4 %copy-start.6 = (bf16[256,1024]{1,0:T(8,128)(2,1)}, bf16[256,1024]{1,0:T(8,128)(2,1)S(1)}, u32[]{:S(2)}) copy-start(bf16[256,1024]{1,0:T(8,128)(2,1)S(1)} %collective-permute-done.10) | copy-start | bytes 1572868
  79.8 25.0 %collective-permute-start.12 = (bf16[256,1024]{1,0:T(8,128)(2,1)}, bf16[256,1024]{1,0:T(8,128)(2,1)}, u32[]{:S(2)}, u32[]{:S(2)}) collective-permute-start(bf16[256,1024]{1,0:T(8,128)(2,1)} %fusion.2), channel_id=1, source_target_pairs={{0,2},{1,3},{2,0},{3,1},{4,6},{5,7},{6,4},{7,5},{8,10},{9,11},{10,... | collective-permute-start | bytes 1572872 | tf_op jit(solution)/shard_map/ppermute | solution.py:18
  91.2 16.1 %all-to-all-start.1 = ((bf16[8,48,1024]{2,1,0:T(8,128)(2,1)}), bf16[8,48,1024]{2,1,0:T(8,128)(2,1)S(1)}, u32[]{:S(2)}, u32[]{:S(2)}) async-start(bf16[8,48,1024]{2,1,0:T(8,128)(2,1)} %bitcast.61), calls=%async_computation.1 | async-start | bytes 1572864 | tf_op jit(solution)/shard_map/all_to_all | solution.py:264
  (6 other events, 15.8 us)
where the time goes:
time: 109 us
  waiting for transfers between devices  40 us (37%)
  starting transfers between devices  39 us (36%)
  other arithmetic  15.2 us (14%)
  matrix products  7.16 us (7%)
  between operations  6.19 us (6%)
    ppermute x5, waiting for transfers between devices, from_partner(): return lax.ppermute(value, 'rep', pairs)  30.9 us
    ppermute x5, starting transfers between devices, from_partner(): return lax.ppermute(value, 'rep', pairs)  18 us
    ppermute x1, waiting for transfers between devices, handed_down(): self.four = lax.ppermute(send, 'rep', OUTWARD)  7.01 us
    ppermute x1, starting transfers between devices, forward(): self.up_side = lax.ppermute(self.up, 'rep', INWARD)  5.09 us
    all_to_all x1, starting transfers between devices, on_device(): lax.all_to_all(dispatched, 'section', split_axis=0, concat_axis=0, tiled=...  3.72 us
    all_to_all x1, starting transfers between devices, on_device(): lax.all_to_all(slot_grad, 'section', split_axis=0, concat_axis=0, tiled=T...  3.55 us
    dot_general x1, matrix products, on_device(): lax.dot_general(selector, token_rows, (((0,), (0,)), ((), ())), preferred...  2.43 us
    sub x1, other arithmetic, on_device(): slow_float - pull * outer_here  2.39 us
  transfers between devices with their start and end apart: 15, of which 7 were waited for; matrix products, arithmetic and copies ran while one was open for 20% of the time, Pallas kernels for 0%

commit v1 on v0

--- a/solution.py
+++ b/solution.py
@@ -104,9 +104,12 @@
         return jnp.where(self.inner, up_in, two)
 
     def gate_here(self, earlier):
+        self.three, gate_in = lax.optimization_barrier((self.three, self.gate_in, *earlier))[:2]
+        return jnp.where(self.inner, gate_in, self.three)
+
+    def static_in(self, earlier):
         three = after(self.three, *earlier)
-        static_in = jnp.where(self.inner, three, self.one)
-        return lax.optimization_barrier(jnp.where(self.inner, self.gate_in, three)), static_in
+        return side_by_side(jnp.where(self.inner, three, self.one))
 
     def swap_down(self, earlier):
         second = after(self.second_down, *earlier)
@@ -190,8 +193,7 @@
 
     up_act = jnp.dot(rows, up_mat, preferred_element_type=jnp.float32)
     if line is not None:
-        gate_mat, static_in = line.gate_here((up_act,))
-        static_in = side_by_side(static_in)
+        gate_mat = line.gate_here((up_act,))
     gate_act = jnp.dot(rows, gate_mat, preferred_element_type=jnp.float32)
     sigmoid_gate = jax.nn.sigmoid(gate_act)
     hidden = (gate_act * sigmoid_gate * up_act).astype(jnp.bfloat16)
@@ -209,7 +211,7 @@
     down_grad_in = from_partner(down_grad, 0)
     if line is not None:
         sent = line.handed_down((down_grad,))
-        static_in = after(static_in, sent)
+        static_in = line.static_in((sent,))
         down_grad_in = after(down_grad_in, static_in)
     own_routed, match_routed, static_routed = down_grad, down_grad, static_part
     for index in lower:

time: 109 us -> 109 us (level)
  waiting for transfers between devices: 40 us -> 36.6 us
  other arithmetic: 15.2 us -> 17.2 us
  starting transfers between devices: 39 us -> 40.1 us
    ppermute x5, waiting for transfers between devices: 30.9 us -> 29.3 us  [from_partner(): return lax.ppermute(value, 'rep', pairs)]
  transfers between devices with their start and end apart: 15 -> 15, of which waited for: 7 -> 7; matrix products, arithmetic and copies ran while one was open for 20% -> 22% of each run, Pallas kernels for 0% -> 0%
where the time goes in v1:
time: 109 us; the launch traced here: 108 us
  starting transfers between devices  40.1 us (37%)
  waiting for transfers between devices  36.6 us (34%)
  other arithmetic  17.2 us (16%)
  matrix products  7.23 us (7%)
  between operations  6.18 us (6%)
    ppermute x5, waiting for transfers between devices, from_partner(): return lax.ppermute(value, 'rep', pairs)  29.3 us
    ppermute x5, starting transfers between devices, from_partner(): return lax.ppermute(value, 'rep', pairs)  18.9 us
    ppermute x1, waiting for transfers between devices, handed_down(): self.four = lax.ppermute(send, 'rep', OUTWARD)  6.57 us
    ppermute x1, starting transfers between devices, forward(): self.up_side = lax.ppermute(self.up, 'rep', INWARD)  5.09 us
    all_to_all x1, starting transfers between devices, on_device(): lax.all_to_all(dispatched, 'section', split_axis=0, concat_axis=0, tiled=...  3.73 us
    all_to_all x1, starting transfers between devices, on_device(): lax.all_to_all(slot_grad, 'section', split_axis=0, concat_axis=0, tiled=T...  3.68 us
    dot_general x1, matrix products, on_device(): lax.dot_general(selector, token_rows, (((0,), (0,)), ((), ())), preferred...  2.44 us
    sub x1, other arithmetic, on_device(): slow_float - pull * outer_here  2.23 us
  transfers between devices with their start and end apart: 15, of which 7 were waited for; matrix products, arithmetic and copies ran while one was open for 22% of the time, Pallas kernels for 0%

profile of v1, /device:TPU:0, one launch (start us, length us, event | category | flops | bytes accessed | tf_op | source)
XLA Modules:
  0.0 108.3 jit_solution(17671225659547672055)
XLA Ops:
  0.7 5.1 %collective-permute-start = (bf16[1024,256]{1,0:T(8,128)(2,1)}, bf16[1024,256]{1,0:T(8,128)(2,1)S(1)}, u32[]{:S(2)}, u32[]{:S(2)}) collective-permute-start(bf16[1024,256]{1,0:T(8,128)(2,1)} %bitcast.60), channel_id=1, source_target_pairs={{0,1},{3,2},{4,5},{7,6},{8,9},{11,10},{12,13},{15,14},{16,17},{19,... | collective-permute-start | bytes 1572872 | tf_op jit(solution)/shard_map/ppermute | solution.py:63
  5.8 1.5 %collective-permute-start.2 = (bf16[1024,256]{1,0:T(8,128)(2,1)}, bf16[1024,256]{1,0:T(8,128)(2,1)}, u32[]{:S(2)}, u32[]{:S(2)}) collective-permute-start(bf16[1024,256]{1,0:T(8,128)(2,1)} %bitcast.61), channel_id=1, source_target_pairs={{1,2},{2,1},{5,6},{6,5},{9,10},{10,9},{13,14},{14,13},{17,18},{18,... | collective-permute-start | bytes 1572872 | tf_op jit(solution)/shard_map/ppermute | solution.py:64
  13.7 1.4 %subtract_convert_fusion.1 = bf16[256,1024]{1,0:T(8,128)(2,1)S(1)} fusion(bf16[1,1,256,1024]{3,2,1,0:T(8,128)(2,1)} %param.17, bf16[1,1,256,1024]{3,2,1,0:T(8,128)(2,1)} %param.16), kind=kLoop, calls=%fused_computation.26 | loop fusion | flops 1572864 | bytes 1572864 | tf_op jit(solution)/shard_map/convert_element_type | solution.py:161
  16.2 1.4 %collective-permute-start.4 = (bf16[1024,256]{1,0:T(8,128)(2,1)}, bf16[1024,256]{1,0:T(8,128)(2,1)}, u32[]{:S(2)}, u32[]{:S(2)}) collective-permute-start(bf16[1024,256]{1,0:T(8,128)(2,1)} %broadcast_select_fusion.3), channel_id=1, source_target_pairs={{0,1},{1,0},{2,3},{3,2},{4,5},{5,4},{6,7},{7,6},{8,9},{9,8},{10,11... | collective-permute-start | bytes 1572872 | tf_op jit(solution)/shard_map/ppermute | solution.py:18
  19.7 1.6 %collective-permute-start.1 = (bf16[1024,256]{1,0:T(8,128)(2,1)}, bf16[1024,256]{1,0:T(8,128)(2,1)}, u32[]{:S(2)}, u32[]{:S(2)}) collective-permute-start(bf16[1024,256]{1,0:T(8,128)(2,1)} %get-tuple-element.65), channel_id=1, source_target_pairs={{1,2},{2,1},{5,6},{6,5},{9,10},{10,9},{13,14},{14,13},{17,18},{18,... | collective-permute-start | bytes 1572872 | tf_op jit(solution)/shard_map/ppermute | solution.py:73
  21.3 2.4 %convolution_convert_fusion = bf16[384,1024]{1,0:T(8,128)(2,1)} fusion(bf16[1,1,256,1024]{3,2,1,0:T(8,128)(2,1)} %param.10, s32[256]{0:T(256)S(1)} %multiply_add_fusion), kind=kOutput, calls=%fused_computation.1 | convolution fusion | flops 201818112 | bytes 1311744 | tf_op jit(solution)/shard_map/dot_general | solution.py:164
  23.7 3.7 %all-to-all-start = ((bf16[8,48,1024]{2,1,0:T(8,128)(2,1)}), bf16[8,48,1024]{2,1,0:T(8,128)(2,1)S(1)}, u32[]{:S(2)}, u32[]{:S(2)}) async-start(bf16[8,48,1024]{2,1,0:T(8,128)(2,1)} %bitcast.16), calls=%async_computation | async-start | bytes 1572864 | tf_op jit(solution)/shard_map/all_to_all | solution.py:183
  27.4 2.4 %collective-permute-done.4 = bf16[1024,256]{1,0:T(8,128)(2,1)} collective-permute-done((bf16[1024,256]{1,0:T(8,128)(2,1)}, bf16[1024,256]{1,0:T(8,128)(2,1)}, u32[]{:S(2)}, u32[]{:S(2)}) %collective-permute-start.4) | collective-permute-done | bytes 524320 | tf_op jit(solution)/shard_map/ppermute | solution.py:18
  29.9 1.5 %collective-permute-start.5 = (bf16[1024,256]{1,0:T(8,128)(2,1)}, bf16[1024,256]{1,0:T(8,128)(2,1)}, u32[]{:S(2)}, u32[]{:S(2)}) collective-permute-start(bf16[1024,256]{1,0:T(8,128)(2,1)} %collective-permute-done.4), channel_id=1, source_target_pairs={{1,2},{2,1},{5,6},{6,5},{9,10},{10,9},{13,14},{14,13},{17,18},{18,... | collective-permute-start | bytes 1572872 | tf_op jit(solution)/shard_map/ppermute | solution.py:75
  31.4 2.1 %select_select_fusion.4 = bf16[1024,256]{1,0:T(8,128)(2,1)} fusion(bf16[1024,256]{1,0:T(8,128)(2,1)} %collective-permute-done.1, pred[]{:T(512)} %bitcast.7, pred[]{:T(512)S(6)} %or.3, bf16[1,1,1024,256]{3,2,1,0:T(8,128)(2,1)S(1)} %copy-done.3, bf16[256,256]{1,0:T(8,128)(2,1)S(1)} %get-tuple-element.81, bf16[256,256]{1,0:T(8,128)(2,1)S(1)} %get-tuple-element.82, ...), kind=kLoop, calls=%fused_computation.44 | loop fusion | flops 2621440 | bytes 2097154 | tf_op jit(solution)/shard_map/jit(_where)/select_n | solution.py:81
  33.5 4.5 %collective-permute-start.3 = (bf16[1024,256]{1,0:T(8,128)(2,1)}, bf16[1024,256]{1,0:T(8,128)(2,1)S(1)}, u32[]{:S(2)}, u32[]{:S(2)}) collective-permute-start(bf16[1024,256]{1,0:T(8,128)(2,1)} %select_select_fusion.4), channel_id=1, source_target_pairs={{0,1},{1,0},{2,3},{3,2},{4,5},{5,4},{6,7},{7,6},{8,9},{9,8},{10,11... | collective-permute-start | bytes 1572872 | tf_op jit(solution)/shard_map/ppermute | solution.py:18
  38.0 1.5 %collective-permute-start.7 = (bf16[1024,256]{1,0:T(8,128)(2,1)}, bf16[1024,256]{1,0:T(8,128)(2,1)}, u32[]{:S(2)}, u32[]{:S(2)}) collective-permute-start(bf16[1024,256]{1,0:T(8,128)(2,1)} %get-tuple-element.43), channel_id=1, source_target_pairs={{1,2},{2,1},{5,6},{6,5},{9,10},{10,9},{13,14},{14,13},{17,18},{18,... | collective-permute-start | bytes 1572872 | tf_op jit(solution)/shard_map/ppermute | solution.py:83
  40.0 1.9 %select_select_fusion.2 = (bf16[1024,256]{1,0:T(8,128)(2,1)S(1)}, bf16[1024,256]{1,0:T(8,128)(2,1)S(1)}) fusion(bf16[1024,256]{1,0:T(8,128)(2,1)} %collective-permute-done.4, bf16[1024,256]{1,0:T(8,128)(2,1)} %collective-permute-done.2, bf16[1024,256]{1,0:T(8,128)(2,1)} %collective-permute-done.5, pred[]{:T(512)} %bitcast.8, pred[]{:T(512)} %bitcast.7, ...), kind=kLoop, calls=%fused_computation.42 | loop fusion | flops 3407872 | bytes 3670019 | tf_op jit(solution)/shard_map/jit(_where)/select_n | solution.py:97
  42.0 8.2 %collective-permute-start.6 = (bf16[1024,256]{1,0:T(8,128)(2,1)S(1)}, bf16[1024,256]{1,0:T(8,128)(2,1)S(1)}, u32[]{:S(2)}, u32[]{:S(2)}) collective-permute-start(bf16[1024,256]{1,0:T(8,128)(2,1)S(1)} %get-tuple-element.75), channel_id=1, source_target_pairs={{0,1},{1,0},{2,3},{3,2},{4,5},{5,4},{6,7},{7,6},{8,9},{9,8},{10,11... | collective-permute-start | bytes 1572872 | tf_op jit(solution)/shard_map/ppermute | solution.py:18
  52.7 8.9 %collective-permute-done.6 = bf16[1024,256]{1,0:T(8,128)(2,1)S(1)} collective-permute-done((bf16[1024,256]{1,0:T(8,128)(2,1)S(1)}, bf16[1024,256]{1,0:T(8,128)(2,1)S(1)}, u32[]{:S(2)}, u32[]{:S(2)}) %collective-permute-start.6) | collective-permute-done | bytes 524320 | tf_op jit(solution)/shard_map/ppermute | solution.py:18
  62.6 1.8 %collective-permute-start.10 = (bf16[256,1024]{1,0:T(8,128)(2,1)S(1)}, bf16[256,1024]{1,0:T(8,128)(2,1)S(1)}, u32[]{:S(2)}, u32[]{:S(2)}) collective-permute-start(bf16[256,1024]{1,0:T(8,128)(2,1)S(1)} %convolution_convert_fusion.2), channel_id=1, source_target_pairs={{0,1},{1,0},{2,3},{3,2},{4,5},{5,4},{6,7},{7,6},{8,9},{9,8},{10,11... | collective-permute-start | bytes 1572872 | tf_op jit(solution)/shard_map/ppermute | solution.py:18
  67.7 9.8 %collective-permute-done.10 = bf16[256,1024]{1,0:T(8,128)(2,1)S(1)} collective-permute-done((bf16[256,1024]{1,0:T(8,128)(2,1)S(1)}, bf16[256,1024]{1,0:T(8,128)(2,1)S(1)}, u32[]{:S(2)}, u32[]{:S(2)}) %collective-permute-start.10) | collective-permute-done | bytes 524320 | tf_op jit(solution)/shard_map/ppermute | solution.py:18
  78.8 3.0 %collective-permute-start.12 = (bf16[256,1024]{1,0:T(8,128)(2,1)}, bf16[256,1024]{1,0:T(8,128)(2,1)}, u32[]{:S(2)}, u32[]{:S(2)}) collective-permute-start(bf16[256,1024]{1,0:T(8,128)(2,1)} %fusion.2), channel_id=1, source_target_pairs={{0,2},{1,3},{2,0},{3,1},{4,6},{5,7},{6,4},{7,5},{8,10},{9,11},{10,... | collective-permute-start | bytes 1572872 | tf_op jit(solution)/shard_map/ppermute | solution.py:18
  81.8 6.6 %collective-permute-done.11 = bf16[1024,256]{1,0:T(8,128)(2,1)S(1)} collective-permute-done((bf16[1024,256]{1,0:T(8,128)(2,1)S(1)}, bf16[1024,256]{1,0:T(8,128)(2,1)S(1)}, u32[]{:S(2)}, u32[]{:S(2)}) %collective-permute-start.11) | collective-permute-done | bytes 524320 | tf_op jit(solution)/shard_map/ppermute | solution.py:120
  89.4 1.4 %add_convert_fusion = bf16[384,1024]{1,0:T(8,128)(2,1)} fusion(f32[384,1024]{1,0:T(8,128)S(1)} %fusion.22, bf16[1024,256]{1,0:T(8,128)(2,1)S(1)} %get-tuple-element.46, bf16[1024,256]{1,0:T(8,128)(2,1)S(1)} %collective-permute-done.6, pred[]{:T(512)S(6)} %or.3, f32[384,256]{1,0:T(8,128)S(1)} %fusion.21, f32[384,256]{1,0:T(8,128)S(1)} %convolution_bitcast_fusion, ...), kind=kOutput, calls=%fused_computation | convolution fusion | flops 203358208 | bytes 4587521 | tf_op jit(solution)/shard_map/dot_general | solution.py:262
  90.8 3.7 %all-to-all-start.1 = ((bf16[8,48,1024]{2,1,0:T(8,128)(2,1)}), bf16[8,48,1024]{2,1,0:T(8,128)(2,1)S(1)}, u32[]{:S(2)}, u32[]{:S(2)}) async-start(bf16[8,48,1024]{2,1,0:T(8,128)(2,1)} %bitcast.23), calls=%async_computation.1 | async-start | bytes 1572864 | tf_op jit(solution)/shard_map/all_to_all | solution.py:266
  94.5 2.2 %fusion.11 = f32[256,1024]{1,0:T(8,128)S(1)} fusion(bf16[256,1024]{1,0:T(8,128)(2,1)S(1)} %bitcast.59, bf16[1,1,256,1024]{3,2,1,0:T(8,128)(2,1)} %param.18, pred[]{:T(512)S(6)} %eq.129, pred[]{:T(512)S(6)} %eq.128, pred[]{:T(512)S(6)} %eq.127, bf16[256,1024]{1,0:T(8,128)(2,1)S(1)} %subtract_convert_fusion.1, pred[]{:T(512)} %bitcast.13, ...), kind=kLoop, calls=%fused_computation.24 | loop fusion | flops 8126464 | bytes 4718598 | tf_op jit(solution)/shard_map/sub | solution.py:245
  96.8 8.1 %collective-permute-done.12 = bf16[256,1024]{1,0:T(8,128)(2,1)} collective-permute-done((bf16[256,1024]{1,0:T(8,128)(2,1)}, bf16[256,1024]{1,0:T(8,128)(2,1)}, u32[]{:S(2)}, u32[]{:S(2)}) %collective-permute-start.12) | collective-permute-done | bytes 524320 | tf_op jit(solution)/shard_map/ppermute | solution.py:18
  104.9 2.0 %fusion.12 = bf16[1,1,256,1024]{3,2,1,0:T(8,128)(2,1)} fusion(f32[256,1024]{1,0:T(8,128)S(1)} %fusion.11, bf16[256,1024]{1,0:T(8,128)(2,1)} %collective-permute-done.12), kind=kLoop, calls=%fused_computation.28 | loop fusion | flops 1048576 | bytes 2097152 | tf_op jit(solution)/shard_map/broadcast_in_dim | solution.py:270
  (75 shorter events, 15.4 us)
Async XLA Ops:
  0.6 61.4 %copy-start = (bf16[1,1,8,48,1024]{4,3,2,1,0:T(8,128)(2,1)S(1)}, bf16[1,1,8,48,1024]{4,3,2,1,0:T(8,128)(2,1)}, u32[]{:S(2)}) copy-start(bf16[1,1,8,48,1024]{4,3,2,1,0:T(8,128)(2,1)} %param.19) | copy-start | bytes 2359300
  0.6 14.6 %copy-start.8 = (bf16[1,1,1024,256]{3,2,1,0:T(8,128)(2,1)S(1)}, bf16[1,1,1024,256]{3,2,1,0:T(8,128)(2,1)}, u32[]{:S(2)}) copy-start(bf16[1,1,1024,256]{3,2,1,0:T(8,128)(2,1)} %param.14) | copy-start | bytes 1572868
  0.7 17.8 %collective-permute-start = (bf16[1024,256]{1,0:T(8,128)(2,1)}, bf16[1024,256]{1,0:T(8,128)(2,1)S(1)}, u32[]{:S(2)}, u32[]{:S(2)}) collective-permute-start(bf16[1024,256]{1,0:T(8,128)(2,1)} %bitcast.60), channel_id=1, source_target_pairs={{0,1},{3,2},{4,5},{7,6},{8,9},{11,10},{12,13},{15,14},{16,17},{19,... | collective-permute-start | bytes 1572872 | tf_op jit(solution)/shard_map/ppermute | solution.py:63
  5.8 18.0 %collective-permute-start.2 = (bf16[1024,256]{1,0:T(8,128)(2,1)}, bf16[1024,256]{1,0:T(8,128)(2,1)}, u32[]{:S(2)}, u32[]{:S(2)}) collective-permute-start(bf16[1024,256]{1,0:T(8,128)(2,1)} %bitcast.61), channel_id=1, source_target_pairs={{1,2},{2,1},{5,6},{6,5},{9,10},{10,9},{13,14},{14,13},{17,18},{18,... | collective-permute-start | bytes 1572872 | tf_op jit(solution)/shard_map/ppermute | solution.py:64
  16.2 13.7 %collective-permute-start.4 = (bf16[1024,256]{1,0:T(8,128)(2,1)}, bf16[1024,256]{1,0:T(8,128)(2,1)}, u32[]{:S(2)}, u32[]{:S(2)}) collective-permute-start(bf16[1024,256]{1,0:T(8,128)(2,1)} %broadcast_select_fusion.3), channel_id=1, source_target_pairs={{0,1},{1,0},{2,3},{3,2},{4,5},{5,4},{6,7},{7,6},{8,9},{9,8},{10,11... | collective-permute-start | bytes 1572872 | tf_op jit(solution)/shard_map/ppermute | solution.py:18
  18.5 5.2 %copy-start.4 = (bf16[1024,256]{1,0:T(8,128)(2,1)}, bf16[1024,256]{1,0:T(8,128)(2,1)S(1)}, u32[]{:S(2)}) copy-start(bf16[1024,256]{1,0:T(8,128)(2,1)S(1)} %collective-permute-done) | copy-start | bytes 1572868
  19.7 11.7 %copy-start.1 = (bf16[1,1,256,1024]{3,2,1,0:T(8,128)(2,1)S(1)}, bf16[1,1,256,1024]{3,2,1,0:T(8,128)(2,1)}, u32[]{:S(2)}) copy-start(bf16[1,1,256,1024]{3,2,1,0:T(8,128)(2,1)} %param.16) | copy-start | bytes 1572868
  19.7 11.7 %collective-permute-start.1 = (bf16[1024,256]{1,0:T(8,128)(2,1)}, bf16[1024,256]{1,0:T(8,128)(2,1)}, u32[]{:S(2)}, u32[]{:S(2)}) collective-permute-start(bf16[1024,256]{1,0:T(8,128)(2,1)} %get-tuple-element.65), channel_id=1, source_target_pairs={{1,2},{2,1},{5,6},{6,5},{9,10},{10,9},{13,14},{14,13},{17,18},{18,... | collective-permute-start | bytes 1572872 | tf_op jit(solution)/shard_map/ppermute | solution.py:73
  23.7 16.3 %all-to-all-start = ((bf16[8,48,1024]{2,1,0:T(8,128)(2,1)}), bf16[8,48,1024]{2,1,0:T(8,128)(2,1)S(1)}, u32[]{:S(2)}, u32[]{:S(2)}) async-start(bf16[8,48,1024]{2,1,0:T(8,128)(2,1)} %bitcast.16), calls=%async_computation | async-start | bytes 1572864 | tf_op jit(solution)/shard_map/all_to_all | solution.py:183
  29.9 9.6 %collective-permute-start.5 = (bf16[1024,256]{1,0:T(8,128)(2,1)}, bf16[1024,256]{1,0:T(8,128)(2,1)}, u32[]{:S(2)}, u32[]{:S(2)}) collective-permute-start(bf16[1024,256]{1,0:T(8,128)(2,1)} %collective-permute-done.4), channel_id=1, source_target_pairs={{1,2},{2,1},{5,6},{6,5},{9,10},{10,9},{13,14},{14,13},{17,18},{18,... | collective-permute-start | bytes 1572872 | tf_op jit(solution)/shard_map/ppermute | solution.py:75
  33.5 16.7 %collective-permute-start.3 = (bf16[1024,256]{1,0:T(8,128)(2,1)}, bf16[1024,256]{1,0:T(8,128)(2,1)S(1)}, u32[]{:S(2)}, u32[]{:S(2)}) collective-permute-start(bf16[1024,256]{1,0:T(8,128)(2,1)} %select_select_fusion.4), channel_id=1, source_target_pairs={{0,1},{1,0},{2,3},{3,2},{4,5},{5,4},{6,7},{7,6},{8,9},{9,8},{10,11... | collective-permute-start | bytes 1572872 | tf_op jit(solution)/shard_map/ppermute | solution.py:18
  38.0 13.1 %collective-permute-start.7 = (bf16[1024,256]{1,0:T(8,128)(2,1)}, bf16[1024,256]{1,0:T(8,128)(2,1)}, u32[]{:S(2)}, u32[]{:S(2)}) collective-permute-start(bf16[1024,256]{1,0:T(8,128)(2,1)} %get-tuple-element.43), channel_id=1, source_target_pairs={{1,2},{2,1},{5,6},{6,5},{9,10},{10,9},{13,14},{14,13},{17,18},{18,... | collective-permute-start | bytes 1572872 | tf_op jit(solution)/shard_map/ppermute | solution.py:83
  40.0 10.2 %copy-start.10 = (bf16[256,256]{1,0:T(8,128)(2,1)S(1)}, bf16[256,256]{1,0:T(8,128)(2,1)}, u32[]{:S(2)}) copy-start(bf16[256,256]{1,0:T(8,128)(2,1)} %copy-done.9) | copy-start | bytes 393220
  42.0 9.1 %copy-start.5 = (bf16[1024,256]{1,0:T(8,128)(2,1)S(1)}, bf16[1024,256]{1,0:T(8,128)(2,1)}, u32[]{:S(2)}) copy-start(bf16[1024,256]{1,0:T(8,128)(2,1)} %copy-done.4) | copy-start | bytes 1572868
  42.0 19.6 %collective-permute-start.6 = (bf16[1024,256]{1,0:T(8,128)(2,1)S(1)}, bf16[1024,256]{1,0:T(8,128)(2,1)S(1)}, u32[]{:S(2)}, u32[]{:S(2)}) collective-permute-start(bf16[1024,256]{1,0:T(8,128)(2,1)S(1)} %get-tuple-element.75), channel_id=1, source_target_pairs={{0,1},{1,0},{2,3},{3,2},{4,5},{5,4},{6,7},{7,6},{8,9},{9,8},{10,11... | collective-permute-start | bytes 1572872 | tf_op jit(solution)/shard_map/ppermute | solution.py:18
  50.4 14.6 %collective-permute-start.9 = (bf16[1024,256]{1,0:T(8,128)(2,1)S(1)}, bf16[1024,256]{1,0:T(8,128)(2,1)S(1)}, u32[]{:S(2)}, u32[]{:S(2)}) collective-permute-start(bf16[1024,256]{1,0:T(8,128)(2,1)S(1)} %get-tuple-element.63), channel_id=1, source_target_pairs={{1,2},{2,1},{5,6},{6,5},{9,10},{10,9},{13,14},{14,13},{17,18},{18,... | collective-permute-start | bytes 1572872 | tf_op jit(solution)/shard_map/ppermute | solution.py:96
  62.5 26.0 %copy-start.6 = (bf16[256,1024]{1,0:T(8,128)(2,1)}, bf16[256,1024]{1,0:T(8,128)(2,1)S(1)}, u32[]{:S(2)}) copy-start(bf16[256,1024]{1,0:T(8,128)(2,1)S(1)} %convolution_convert_fusion.2) | copy-start | bytes 1572868
  62.6 14.9 %collective-permute-start.10 = (bf16[256,1024]{1,0:T(8,128)(2,1)S(1)}, bf16[256,1024]{1,0:T(8,128)(2,1)S(1)}, u32[]{:S(2)}, u32[]{:S(2)}) collective-permute-start(bf16[256,1024]{1,0:T(8,128)(2,1)S(1)} %convolution_convert_fusion.2), channel_id=1, source_target_pairs={{0,1},{1,0},{2,3},{3,2},{4,5},{5,4},{6,7},{7,6},{8,9},{9,8},{10,11... | collective-permute-start | bytes 1572872 | tf_op jit(solution)/shard_map/ppermute | solution.py:18
  64.3 14.5 %collective-permute-start.8 = (bf16[1024,256]{1,0:T(8,128)(2,1)S(1)}, bf16[1024,256]{1,0:T(8,128)(2,1)S(1)}, u32[]{:S(2)}, u32[]{:S(2)}) collective-permute-start(bf16[1024,256]{1,0:T(8,128)(2,1)S(1)} %get-tuple-element.48), channel_id=1, source_target_pairs={{1,2},{2,1},{5,6},{6,5},{9,10},{10,9},{13,14},{14,13},{17,18},{18,... | collective-permute-start | bytes 1572872 | tf_op jit(solution)/shard_map/ppermute | solution.py:116
  65.2 23.2 %collective-permute-start.11 = (bf16[1024,256]{1,0:T(8,128)(2,1)S(1)}, bf16[1024,256]{1,0:T(8,128)(2,1)S(1)}, u32[]{:S(2)}, u32[]{:S(2)}) collective-permute-start(bf16[1024,256]{1,0:T(8,128)(2,1)S(1)} %broadcast_select_fusion.8), channel_id=1, source_target_pairs={{1,0},{2,3},{5,4},{6,7},{9,8},{10,11},{13,12},{14,15},{17,16},{18,... | collective-permute-start | bytes 1572872 | tf_op jit(solution)/shard_map/ppermute | solution.py:120
  67.6 20.9 %copy-start.15 = (bf16[256,256]{1,0:T(8,128)(2,1)}, bf16[256,256]{1,0:T(8,128)(2,1)S(1)}, u32[]{:S(2)}) copy-start(bf16[256,256]{1,0:T(8,128)(2,1)S(1)} %get-tuple-element.73) | copy-start | bytes 393220
  77.5 11.1 %copy-start.7 = (bf16[256,1024]{1,0:T(8,128)(2,1)}, bf16[256,1024]{1,0:T(8,128)(2,1)S(1)}, u32[]{:S(2)}) copy-start(bf16[256,1024]{1,0:T(8,128)(2,1)S(1)} %collective-permute-done.10) | copy-start | bytes 1572868
  78.8 26.1 %collective-permute-start.12 = (bf16[256,1024]{1,0:T(8,128)(2,1)}, bf16[256,1024]{1,0:T(8,128)(2,1)}, u32[]{:S(2)}, u32[]{:S(2)}) collective-permute-start(bf16[256,1024]{1,0:T(8,128)(2,1)} %fusion.2), channel_id=1, source_target_pairs={{0,2},{1,3},{2,0},{3,1},{4,6},{5,7},{6,4},{7,5},{8,10},{9,11},{10,... | collective-permute-start | bytes 1572872 | tf_op jit(solution)/shard_map/ppermute | solution.py:18
  90.8 16.2 %all-to-all-start.1 = ((bf16[8,48,1024]{2,1,0:T(8,128)(2,1)}), bf16[8,48,1024]{2,1,0:T(8,128)(2,1)S(1)}, u32[]{:S(2)}, u32[]{:S(2)}) async-start(bf16[8,48,1024]{2,1,0:T(8,128)(2,1)} %bitcast.23), calls=%async_computation.1 | async-start | bytes 1572864 | tf_op jit(solution)/shard_map/all_to_all | solution.py:266
  (8 other events, 21.4 us)

commit v2 on v1

--- a/solution.py
+++ b/solution.py
@@ -68,8 +68,8 @@
         send = lax.optimization_barrier(jnp.where(inner, self.static_part, self.gate))
         self.one = from_partner(send, 0)
         side, self.near, self.far = lax.optimization_barrier((self.up_side, self.near, self.far))
-        first = jnp.where(self.far, side, self.up)
-        second = jnp.where(self.far, self.up, side)
+        first = lax.optimization_barrier(jnp.where(self.far, side, self.up))
+        second = jnp.where(self.far, self.up, after(side, first))
         first_in = lax.ppermute(first, "rep", ACROSS)
         self.quiet, self.first_in = first, first_in
         self.gate_edge = lax.ppermute(self.one, "rep", ACROSS)
@@ -176,9 +176,9 @@
             own_mask,
         )
         bits = line.forward(bits)
-        dispatched, line.gate_hub = lax.optimization_barrier(
-            (dispatched, line.gate_hub, line.quiet)
-        )[:2]
+        dispatched, line.gate_hub, line.second = lax.optimization_barrier(
+            (dispatched, line.gate_hub, line.second, line.quiet)
+        )[:3]
         line.handed_up((dispatched,))
     arrived = lax.all_to_all(dispatched, "section", split_axis=0, concat_axis=0, tiled=True)
     rows = arrived.reshape(-1, model_width)

time: 109 us -> 108 us (level)
  starting transfers between devices: 40.1 us -> 43.7 us
  waiting for transfers between devices: 36.6 us -> 34.4 us
  other arithmetic: 17.2 us -> 15.9 us
    ppermute x5, starting transfers between devices: 18.9 us -> 21.6 us  [from_partner(): return lax.ppermute(value, 'rep', pairs)]
    ppermute x1, waiting for transfers between devices: 6.57 us -> 4.27 us  [handed_down(): self.four = lax.ppermute(send, 'rep', OUTWARD)]
    all_to_all x1, starting transfers between devices: 3.68 us -> 4.79 us  [on_device(): lax.all_to_all(slot_grad, 'section', split_axis=0, concat_axis=0, tiled=T...]
  transfers between devices with their start and end apart: 15 -> 15, of which waited for: 7 -> 6; matrix products, arithmetic and copies ran while one was open for 22% -> 20% of each run, Pallas kernels for 0% -> 0%
where the time goes in v2:
time: 108 us; the launch traced here: 107 us
  starting transfers between devices  43.7 us (40%)
  waiting for transfers between devices  34.4 us (32%)
  other arithmetic  15.9 us (15%)
  matrix products  6.19 us (6%)
  between operations  6.16 us (6%)
    ppermute x5, waiting for transfers between devices, from_partner(): return lax.ppermute(value, 'rep', pairs)  28.7 us
    ppermute x5, starting transfers between devices, from_partner(): return lax.ppermute(value, 'rep', pairs)  21.6 us
    ppermute x1, starting transfers between devices, forward(): self.up_side = lax.ppermute(self.up, 'rep', INWARD)  5.09 us
    all_to_all x1, starting transfers between devices, on_device(): lax.all_to_all(slot_grad, 'section', split_axis=0, concat_axis=0, tiled=T...  4.79 us
    ppermute x1, waiting for transfers between devices, handed_down(): self.four = lax.ppermute(send, 'rep', OUTWARD)  4.27 us
    all_to_all x1, starting transfers between devices, on_device(): lax.all_to_all(dispatched, 'section', split_axis=0, concat_axis=0, tiled=...  3.72 us
    sub x1, other arithmetic, on_device(): slow_float - pull * outer_here  2.23 us
  transfers between devices with their start and end apart: 15, of which 6 were waited for; matrix products, arithmetic and copies ran while one was open for 20% of the time, Pallas kernels for 0%

profile of v2, /device:TPU:0, one launch (start us, length us, event | category | flops | bytes accessed | tf_op | source)
XLA Modules:
  0.0 107.4 jit_solution(16358383225564357311)
XLA Ops:
  0.7 5.1 %collective-permute-start = (bf16[1024,256]{1,0:T(8,128)(2,1)}, bf16[1024,256]{1,0:T(8,128)(2,1)S(1)}, u32[]{:S(2)}, u32[]{:S(2)}) collective-permute-start(bf16[1024,256]{1,0:T(8,128)(2,1)} %bitcast.58), channel_id=1, source_target_pairs={{0,1},{3,2},{4,5},{7,6},{8,9},{11,10},{12,13},{15,14},{16,17},{19,... | collective-permute-start | bytes 1572872 | tf_op jit(solution)/shard_map/ppermute | solution.py:63
  5.8 1.5 %collective-permute-start.2 = (bf16[1024,256]{1,0:T(8,128)(2,1)}, bf16[1024,256]{1,0:T(8,128)(2,1)}, u32[]{:S(2)}, u32[]{:S(2)}) collective-permute-start(bf16[1024,256]{1,0:T(8,128)(2,1)} %bitcast.62), channel_id=1, source_target_pairs={{1,2},{2,1},{5,6},{6,5},{9,10},{10,9},{13,14},{14,13},{17,18},{18,... | collective-permute-start | bytes 1572872 | tf_op jit(solution)/shard_map/ppermute | solution.py:64
  13.7 1.4 %subtract_convert_fusion.1 = bf16[256,1024]{1,0:T(8,128)(2,1)S(1)} fusion(bf16[1,1,256,1024]{3,2,1,0:T(8,128)(2,1)} %param.17, bf16[1,1,256,1024]{3,2,1,0:T(8,128)(2,1)} %param.16), kind=kLoop, calls=%fused_computation.26 | loop fusion | flops 1572864 | bytes 1572864 | tf_op jit(solution)/shard_map/convert_element_type | solution.py:161
  16.2 1.4 %collective-permute-start.4 = (bf16[1024,256]{1,0:T(8,128)(2,1)}, bf16[1024,256]{1,0:T(8,128)(2,1)}, u32[]{:S(2)}, u32[]{:S(2)}) collective-permute-start(bf16[1024,256]{1,0:T(8,128)(2,1)} %broadcast_select_fusion.3), channel_id=1, source_target_pairs={{0,1},{1,0},{2,3},{3,2},{4,5},{5,4},{6,7},{7,6},{8,9},{9,8},{10,11... | collective-permute-start | bytes 1572872 | tf_op jit(solution)/shard_map/ppermute | solution.py:18
  19.4 1.5 %collective-permute-start.1 = (bf16[1024,256]{1,0:T(8,128)(2,1)}, bf16[1024,256]{1,0:T(8,128)(2,1)}, u32[]{:S(2)}, u32[]{:S(2)}) collective-permute-start(bf16[1024,256]{1,0:T(8,128)(2,1)} %broadcast_select_fusion.7), channel_id=1, source_target_pairs={{1,2},{2,1},{5,6},{6,5},{9,10},{10,9},{13,14},{14,13},{17,18},{18,... | collective-permute-start | bytes 1572872 | tf_op jit(solution)/shard_map/ppermute | solution.py:73
  20.9 1.4 %convolution_convert_fusion = bf16[384,1024]{1,0:T(8,128)(2,1)} fusion(bf16[1,1,256,1024]{3,2,1,0:T(8,128)(2,1)S(1)} %copy-done.16, s32[256]{0:T(256)S(1)} %multiply_add_fusion), kind=kOutput, calls=%fused_computation.1 | convolution fusion | flops 201818112 | bytes 1311744 | tf_op jit(solution)/shard_map/dot_general | solution.py:164
  23.2 3.7 %all-to-all-start = ((bf16[8,48,1024]{2,1,0:T(8,128)(2,1)}), bf16[8,48,1024]{2,1,0:T(8,128)(2,1)S(1)}, u32[]{:S(2)}, u32[]{:S(2)}) async-start(bf16[8,48,1024]{2,1,0:T(8,128)(2,1)} %bitcast.59), calls=%async_computation | async-start | bytes 1572864 | tf_op jit(solution)/shard_map/all_to_all | solution.py:183
  26.9 3.0 %collective-permute-done.4 = bf16[1024,256]{1,0:T(8,128)(2,1)} collective-permute-done((bf16[1024,256]{1,0:T(8,128)(2,1)}, bf16[1024,256]{1,0:T(8,128)(2,1)}, u32[]{:S(2)}, u32[]{:S(2)}) %collective-permute-start.4) | collective-permute-done | bytes 524320 | tf_op jit(solution)/shard_map/ppermute | solution.py:18
  29.9 1.5 %collective-permute-start.5 = (bf16[1024,256]{1,0:T(8,128)(2,1)}, bf16[1024,256]{1,0:T(8,128)(2,1)}, u32[]{:S(2)}, u32[]{:S(2)}) collective-permute-start(bf16[1024,256]{1,0:T(8,128)(2,1)} %collective-permute-done.4), channel_id=1, source_target_pairs={{1,2},{2,1},{5,6},{6,5},{9,10},{10,9},{13,14},{14,13},{17,18},{18,... | collective-permute-start | bytes 1572872 | tf_op jit(solution)/shard_map/ppermute | solution.py:75
  32.4 4.2 %collective-permute-start.3 = (bf16[1024,256]{1,0:T(8,128)(2,1)}, bf16[1024,256]{1,0:T(8,128)(2,1)S(1)}, u32[]{:S(2)}, u32[]{:S(2)}) collective-permute-start(bf16[1024,256]{1,0:T(8,128)(2,1)} %select_select_fusion.4), channel_id=1, source_target_pairs={{0,1},{1,0},{2,3},{3,2},{4,5},{5,4},{6,7},{7,6},{8,9},{9,8},{10,11... | collective-permute-start | bytes 1572872 | tf_op jit(solution)/shard_map/ppermute | solution.py:18
  36.6 1.5 %collective-permute-start.7 = (bf16[1024,256]{1,0:T(8,128)(2,1)}, bf16[1024,256]{1,0:T(8,128)(2,1)}, u32[]{:S(2)}, u32[]{:S(2)}) collective-permute-start(bf16[1024,256]{1,0:T(8,128)(2,1)} %broadcast_select_fusion.6), channel_id=1, source_target_pairs={{1,2},{2,1},{5,6},{6,5},{9,10},{10,9},{13,14},{14,13},{17,18},{18,... | collective-permute-start | bytes 1572872 | tf_op jit(solution)/shard_map/ppermute | solution.py:83
  38.1 1.4 %all-to-all-done = bf16[8,48,1024]{2,1,0:T(8,128)(2,1)S(1)} async-done(((bf16[8,48,1024]{2,1,0:T(8,128)(2,1)}), bf16[8,48,1024]{2,1,0:T(8,128)(2,1)S(1)}, u32[]{:S(2)}, u32[]{:S(2)}) %all-to-all-start) | async-done | bytes 786464 | tf_op jit(solution)/shard_map/all_to_all | solution.py:183
  39.5 2.1 %select_select_fusion.2 = (bf16[1024,256]{1,0:T(8,128)(2,1)S(1)}, bf16[1024,256]{1,0:T(8,128)(2,1)S(1)}) fusion(bf16[1024,256]{1,0:T(8,128)(2,1)} %collective-permute-done.4, bf16[1024,256]{1,0:T(8,128)(2,1)} %collective-permute-done.2, bf16[1024,256]{1,0:T(8,128)(2,1)} %collective-permute-done.5, pred[]{:T(512)} %bitcast.8, pred[]{:T(512)} %bitcast.7, ...), kind=kLoop, calls=%fused_computation.42 | loop fusion | flops 3407872 | bytes 3670019 | tf_op jit(solution)/shard_map/jit(_where)/select_n | solution.py:97
  41.6 8.8 %collective-permute-start.6 = (bf16[1024,256]{1,0:T(8,128)(2,1)S(1)}, bf16[1024,256]{1,0:T(8,128)(2,1)S(1)}, u32[]{:S(2)}, u32[]{:S(2)}) collective-permute-start(bf16[1024,256]{1,0:T(8,128)(2,1)S(1)} %get-tuple-element.77), channel_id=1, source_target_pairs={{0,1},{1,0},{2,3},{3,2},{4,5},{5,4},{6,7},{7,6},{8,9},{9,8},{10,11... | collective-permute-start | bytes 1572872 | tf_op jit(solution)/shard_map/ppermute | solution.py:18
  51.8 8.7 %collective-permute-done.6 = bf16[1024,256]{1,0:T(8,128)(2,1)S(1)} collective-permute-done((bf16[1024,256]{1,0:T(8,128)(2,1)S(1)}, bf16[1024,256]{1,0:T(8,128)(2,1)S(1)}, u32[]{:S(2)}, u32[]{:S(2)}) %collective-permute-start.6) | collective-permute-done | bytes 524320 | tf_op jit(solution)/shard_map/ppermute | solution.py:18
  61.5 1.8 %collective-permute-start.10 = (bf16[256,1024]{1,0:T(8,128)(2,1)S(1)}, bf16[256,1024]{1,0:T(8,128)(2,1)S(1)}, u32[]{:S(2)}, u32[]{:S(2)}) collective-permute-start(bf16[256,1024]{1,0:T(8,128)(2,1)S(1)} %convolution_convert_fusion.2), channel_id=1, source_target_pairs={{0,1},{1,0},{2,3},{3,2},{4,5},{5,4},{6,7},{7,6},{8,9},{9,8},{10,11... | collective-permute-start | bytes 1572872 | tf_op jit(solution)/shard_map/ppermute | solution.py:18
  66.6 8.1 %collective-permute-done.10 = bf16[256,1024]{1,0:T(8,128)(2,1)S(1)} collective-permute-done((bf16[256,1024]{1,0:T(8,128)(2,1)S(1)}, bf16[256,1024]{1,0:T(8,128)(2,1)S(1)}, u32[]{:S(2)}, u32[]{:S(2)}) %collective-permute-start.10) | collective-permute-done | bytes 524320 | tf_op jit(solution)/shard_map/ppermute | solution.py:18
  76.0 5.4 %collective-permute-start.12 = (bf16[256,1024]{1,0:T(8,128)(2,1)}, bf16[256,1024]{1,0:T(8,128)(2,1)}, u32[]{:S(2)}, u32[]{:S(2)}) collective-permute-start(bf16[256,1024]{1,0:T(8,128)(2,1)} %fusion.2), channel_id=1, source_target_pairs={{0,2},{1,3},{2,0},{3,1},{4,6},{5,7},{6,4},{7,5},{8,10},{9,11},{10,... | collective-permute-start | bytes 1572872 | tf_op jit(solution)/shard_map/ppermute | solution.py:18
  81.4 4.3 %collective-permute-done.11 = bf16[1024,256]{1,0:T(8,128)(2,1)S(1)} collective-permute-done((bf16[1024,256]{1,0:T(8,128)(2,1)S(1)}, bf16[1024,256]{1,0:T(8,128)(2,1)S(1)}, u32[]{:S(2)}, u32[]{:S(2)}) %collective-permute-start.11) | collective-permute-done | bytes 524320 | tf_op jit(solution)/shard_map/ppermute | solution.py:120
  86.8 1.4 %add_convert_fusion = bf16[384,1024]{1,0:T(8,128)(2,1)} fusion(f32[384,1024]{1,0:T(8,128)S(1)} %fusion.22, bf16[1024,256]{1,0:T(8,128)(2,1)S(1)} %get-tuple-element.50, bf16[1024,256]{1,0:T(8,128)(2,1)S(1)} %collective-permute-done.6, pred[]{:T(512)S(6)} %or.3, f32[384,256]{1,0:T(8,128)S(1)} %fusion.21, f32[384,256]{1,0:T(8,128)S(1)} %convolution_bitcast_fusion, ...), kind=kOutput, calls=%fused_computation | convolution fusion | flops 203358208 | bytes 4587521 | tf_op jit(solution)/shard_map/dot_general | solution.py:262
  88.2 4.8 %all-to-all-start.1 = ((bf16[8,48,1024]{2,1,0:T(8,128)(2,1)}), bf16[8,48,1024]{2,1,0:T(8,128)(2,1)S(1)}, u32[]{:S(2)}, u32[]{:S(2)}) async-start(bf16[8,48,1024]{2,1,0:T(8,128)(2,1)} %bitcast.23), calls=%async_computation.1 | async-start | bytes 1572864 | tf_op jit(solution)/shard_map/all_to_all | solution.py:266
  93.0 2.2 %fusion.11 = f32[256,1024]{1,0:T(8,128)S(1)} fusion(bf16[256,1024]{1,0:T(8,128)(2,1)S(1)} %bitcast.61, bf16[1,1,256,1024]{3,2,1,0:T(8,128)(2,1)} %param.18, pred[]{:T(512)S(6)} %eq.129, pred[]{:T(512)S(6)} %eq.128, pred[]{:T(512)S(6)} %eq.127, bf16[256,1024]{1,0:T(8,128)(2,1)S(1)} %subtract_convert_fusion.1, pred[]{:T(512)} %bitcast.13, ...), kind=kLoop, calls=%fused_computation.24 | loop fusion | flops 8126464 | bytes 4718598 | tf_op jit(solution)/shard_map/sub | solution.py:245
  95.2 8.9 %collective-permute-done.12 = bf16[256,1024]{1,0:T(8,128)(2,1)} collective-permute-done((bf16[256,1024]{1,0:T(8,128)(2,1)}, bf16[256,1024]{1,0:T(8,128)(2,1)}, u32[]{:S(2)}, u32[]{:S(2)}) %collective-permute-start.12) | collective-permute-done | bytes 524320 | tf_op jit(solution)/shard_map/ppermute | solution.py:18
  104.1 2.0 %fusion.12 = bf16[1,1,256,1024]{3,2,1,0:T(8,128)(2,1)} fusion(f32[256,1024]{1,0:T(8,128)S(1)} %fusion.11, bf16[256,1024]{1,0:T(8,128)(2,1)} %collective-permute-done.12), kind=kLoop, calls=%fused_computation.28 | loop fusion | flops 1048576 | bytes 2097152 | tf_op jit(solution)/shard_map/broadcast_in_dim | solution.py:270
  (78 shorter events, 15.3 us)
Async XLA Ops:
  0.6 60.3 %copy-start = (bf16[1,1,8,48,1024]{4,3,2,1,0:T(8,128)(2,1)S(1)}, bf16[1,1,8,48,1024]{4,3,2,1,0:T(8,128)(2,1)}, u32[]{:S(2)}) copy-start(bf16[1,1,8,48,1024]{4,3,2,1,0:T(8,128)(2,1)} %param.19) | copy-start | bytes 2359300
  0.6 14.6 %copy-start.8 = (bf16[1,1,1024,256]{3,2,1,0:T(8,128)(2,1)S(1)}, bf16[1,1,1024,256]{3,2,1,0:T(8,128)(2,1)}, u32[]{:S(2)}) copy-start(bf16[1,1,1024,256]{3,2,1,0:T(8,128)(2,1)} %param.14) | copy-start | bytes 1572868
  0.7 17.8 %collective-permute-start = (bf16[1024,256]{1,0:T(8,128)(2,1)}, bf16[1024,256]{1,0:T(8,128)(2,1)S(1)}, u32[]{:S(2)}, u32[]{:S(2)}) collective-permute-start(bf16[1024,256]{1,0:T(8,128)(2,1)} %bitcast.58), channel_id=1, source_target_pairs={{0,1},{3,2},{4,5},{7,6},{8,9},{11,10},{12,13},{15,14},{16,17},{19,... | collective-permute-start | bytes 1572872 | tf_op jit(solution)/shard_map/ppermute | solution.py:63
  5.8 17.4 %collective-permute-start.2 = (bf16[1024,256]{1,0:T(8,128)(2,1)}, bf16[1024,256]{1,0:T(8,128)(2,1)}, u32[]{:S(2)}, u32[]{:S(2)}) collective-permute-start(bf16[1024,256]{1,0:T(8,128)(2,1)} %bitcast.62), channel_id=1, source_target_pairs={{1,2},{2,1},{5,6},{6,5},{9,10},{10,9},{13,14},{14,13},{17,18},{18,... | collective-permute-start | bytes 1572872 | tf_op jit(solution)/shard_map/ppermute | solution.py:64
  16.2 13.7 %collective-permute-start.4 = (bf16[1024,256]{1,0:T(8,128)(2,1)}, bf16[1024,256]{1,0:T(8,128)(2,1)}, u32[]{:S(2)}, u32[]{:S(2)}) collective-permute-start(bf16[1024,256]{1,0:T(8,128)(2,1)} %broadcast_select_fusion.3), channel_id=1, source_target_pairs={{0,1},{1,0},{2,3},{3,2},{4,5},{5,4},{6,7},{7,6},{8,9},{9,8},{10,11... | collective-permute-start | bytes 1572872 | tf_op jit(solution)/shard_map/ppermute | solution.py:18
  19.4 11.9 %collective-permute-start.1 = (bf16[1024,256]{1,0:T(8,128)(2,1)}, bf16[1024,256]{1,0:T(8,128)(2,1)}, u32[]{:S(2)}, u32[]{:S(2)}) collective-permute-start(bf16[1024,256]{1,0:T(8,128)(2,1)} %broadcast_select_fusion.7), channel_id=1, source_target_pairs={{1,2},{2,1},{5,6},{6,5},{9,10},{10,9},{13,14},{14,13},{17,18},{18,... | collective-permute-start | bytes 1572872 | tf_op jit(solution)/shard_map/ppermute | solution.py:73
  22.3 9.0 %copy-start.1 = (bf16[1,1,256,1024]{3,2,1,0:T(8,128)(2,1)S(1)}, bf16[1,1,256,1024]{3,2,1,0:T(8,128)(2,1)}, u32[]{:S(2)}) copy-start(bf16[1,1,256,1024]{3,2,1,0:T(8,128)(2,1)} %param.16) | copy-start | bytes 1572868
  23.2 16.3 %all-to-all-start = ((bf16[8,48,1024]{2,1,0:T(8,128)(2,1)}), bf16[8,48,1024]{2,1,0:T(8,128)(2,1)S(1)}, u32[]{:S(2)}, u32[]{:S(2)}) async-start(bf16[8,48,1024]{2,1,0:T(8,128)(2,1)} %bitcast.59), calls=%async_computation | async-start | bytes 1572864 | tf_op jit(solution)/shard_map/all_to_all | solution.py:183
  29.9 8.2 %collective-permute-start.5 = (bf16[1024,256]{1,0:T(8,128)(2,1)}, bf16[1024,256]{1,0:T(8,128)(2,1)}, u32[]{:S(2)}, u32[]{:S(2)}) collective-permute-start(bf16[1024,256]{1,0:T(8,128)(2,1)} %collective-permute-done.4), channel_id=1, source_target_pairs={{1,2},{2,1},{5,6},{6,5},{9,10},{10,9},{13,14},{14,13},{17,18},{18,... | collective-permute-start | bytes 1572872 | tf_op jit(solution)/shard_map/ppermute | solution.py:75
  32.4 18.0 %collective-permute-start.3 = (bf16[1024,256]{1,0:T(8,128)(2,1)}, bf16[1024,256]{1,0:T(8,128)(2,1)S(1)}, u32[]{:S(2)}, u32[]{:S(2)}) collective-permute-start(bf16[1024,256]{1,0:T(8,128)(2,1)} %select_select_fusion.4), channel_id=1, source_target_pairs={{0,1},{1,0},{2,3},{3,2},{4,5},{5,4},{6,7},{7,6},{8,9},{9,8},{10,11... | collective-permute-start | bytes 1572872 | tf_op jit(solution)/shard_map/ppermute | solution.py:18
  36.6 14.7 %collective-permute-start.7 = (bf16[1024,256]{1,0:T(8,128)(2,1)}, bf16[1024,256]{1,0:T(8,128)(2,1)}, u32[]{:S(2)}, u32[]{:S(2)}) collective-permute-start(bf16[1024,256]{1,0:T(8,128)(2,1)} %broadcast_select_fusion.6), channel_id=1, source_target_pairs={{1,2},{2,1},{5,6},{6,5},{9,10},{10,9},{13,14},{14,13},{17,18},{18,... | collective-permute-start | bytes 1572872 | tf_op jit(solution)/shard_map/ppermute | solution.py:83
  39.5 10.9 %copy-start.10 = (bf16[256,256]{1,0:T(8,128)(2,1)S(1)}, bf16[256,256]{1,0:T(8,128)(2,1)}, u32[]{:S(2)}) copy-start(bf16[256,256]{1,0:T(8,128)(2,1)} %copy-done.9) | copy-start | bytes 393220
  41.6 9.7 %copy-start.4 = (bf16[1024,256]{1,0:T(8,128)(2,1)S(1)}, bf16[1024,256]{1,0:T(8,128)(2,1)}, u32[]{:S(2)}) copy-start(bf16[1024,256]{1,0:T(8,128)(2,1)} %copy-done.3) | copy-start | bytes 1572868
  41.6 19.0 %collective-permute-start.6 = (bf16[1024,256]{1,0:T(8,128)(2,1)S(1)}, bf16[1024,256]{1,0:T(8,128)(2,1)S(1)}, u32[]{:S(2)}, u32[]{:S(2)}) collective-permute-start(bf16[1024,256]{1,0:T(8,128)(2,1)S(1)} %get-tuple-element.77), channel_id=1, source_target_pairs={{0,1},{1,0},{2,3},{3,2},{4,5},{5,4},{6,7},{7,6},{8,9},{9,8},{10,11... | collective-permute-start | bytes 1572872 | tf_op jit(solution)/shard_map/ppermute | solution.py:18
  50.6 13.4 %collective-permute-start.9 = (bf16[1024,256]{1,0:T(8,128)(2,1)S(1)}, bf16[1024,256]{1,0:T(8,128)(2,1)S(1)}, u32[]{:S(2)}, u32[]{:S(2)}) collective-permute-start(bf16[1024,256]{1,0:T(8,128)(2,1)S(1)} %get-tuple-element.67), channel_id=1, source_target_pairs={{1,2},{2,1},{5,6},{6,5},{9,10},{10,9},{13,14},{14,13},{17,18},{18,... | collective-permute-start | bytes 1572872 | tf_op jit(solution)/shard_map/ppermute | solution.py:96
  61.5 24.4 %copy-start.6 = (bf16[256,1024]{1,0:T(8,128)(2,1)}, bf16[256,1024]{1,0:T(8,128)(2,1)S(1)}, u32[]{:S(2)}) copy-start(bf16[256,1024]{1,0:T(8,128)(2,1)S(1)} %convolution_convert_fusion.2) | copy-start | bytes 1572868
  61.5 13.2 %collective-permute-start.10 = (bf16[256,1024]{1,0:T(8,128)(2,1)S(1)}, bf16[256,1024]{1,0:T(8,128)(2,1)S(1)}, u32[]{:S(2)}, u32[]{:S(2)}) collective-permute-start(bf16[256,1024]{1,0:T(8,128)(2,1)S(1)} %convolution_convert_fusion.2), channel_id=1, source_target_pairs={{0,1},{1,0},{2,3},{3,2},{4,5},{5,4},{6,7},{7,6},{8,9},{9,8},{10,11... | collective-permute-start | bytes 1572872 | tf_op jit(solution)/shard_map/ppermute | solution.py:18
  63.3 12.7 %collective-permute-start.8 = (bf16[1024,256]{1,0:T(8,128)(2,1)S(1)}, bf16[1024,256]{1,0:T(8,128)(2,1)S(1)}, u32[]{:S(2)}, u32[]{:S(2)}) collective-permute-start(bf16[1024,256]{1,0:T(8,128)(2,1)S(1)} %get-tuple-element.52), channel_id=1, source_target_pairs={{1,2},{2,1},{5,6},{6,5},{9,10},{10,9},{13,14},{14,13},{17,18},{18,... | collective-permute-start | bytes 1572872 | tf_op jit(solution)/shard_map/ppermute | solution.py:116
  64.2 21.6 %collective-permute-start.11 = (bf16[1024,256]{1,0:T(8,128)(2,1)S(1)}, bf16[1024,256]{1,0:T(8,128)(2,1)S(1)}, u32[]{:S(2)}, u32[]{:S(2)}) collective-permute-start(bf16[1024,256]{1,0:T(8,128)(2,1)S(1)} %broadcast_select_fusion.8), channel_id=1, source_target_pairs={{1,0},{2,3},{5,4},{6,7},{9,8},{10,11},{13,12},{14,15},{17,16},{18,... | collective-permute-start | bytes 1572872 | tf_op jit(solution)/shard_map/ppermute | solution.py:120
  66.6 19.2 %copy-start.15 = (bf16[256,256]{1,0:T(8,128)(2,1)}, bf16[256,256]{1,0:T(8,128)(2,1)S(1)}, u32[]{:S(2)}) copy-start(bf16[256,256]{1,0:T(8,128)(2,1)S(1)} %get-tuple-element.75) | copy-start | bytes 393220
  74.7 11.2 %copy-start.7 = (bf16[256,1024]{1,0:T(8,128)(2,1)}, bf16[256,1024]{1,0:T(8,128)(2,1)S(1)}, u32[]{:S(2)}) copy-start(bf16[256,1024]{1,0:T(8,128)(2,1)S(1)} %collective-permute-done.10) | copy-start | bytes 1572868
  76.0 28.1 %collective-permute-start.12 = (bf16[256,1024]{1,0:T(8,128)(2,1)}, bf16[256,1024]{1,0:T(8,128)(2,1)}, u32[]{:S(2)}, u32[]{:S(2)}) collective-permute-start(bf16[256,1024]{1,0:T(8,128)(2,1)} %fusion.2), channel_id=1, source_target_pairs={{0,2},{1,3},{2,0},{3,1},{4,6},{5,7},{6,4},{7,5},{8,10},{9,11},{10,... | collective-permute-start | bytes 1572872 | tf_op jit(solution)/shard_map/ppermute | solution.py:18
  88.2 4.8 %copy-start.5 = (bf16[1,1,256,1024]{3,2,1,0:T(8,128)(2,1)S(1)}, bf16[1,1,256,1024]{3,2,1,0:T(8,128)(2,1)}, u32[]{:S(2)}) copy-start(bf16[1,1,256,1024]{3,2,1,0:T(8,128)(2,1)} %param.17) | copy-start | bytes 1572868
  88.2 17.9 %all-to-all-start.1 = ((bf16[8,48,1024]{2,1,0:T(8,128)(2,1)}), bf16[8,48,1024]{2,1,0:T(8,128)(2,1)S(1)}, u32[]{:S(2)}, u32[]{:S(2)}) async-start(bf16[8,48,1024]{2,1,0:T(8,128)(2,1)} %bitcast.23), calls=%async_computation.1 | async-start | bytes 1572864 | tf_op jit(solution)/shard_map/all_to_all | solution.py:266
  (9 other events, 28.0 us)
